TPU v7x, 256 devices: a whole 4x4x8 slice. The times are simulated.
256 devices in a mesh: src: 128 (over z, y, x), act: 2 (over core).
Axes of the slice: x: 4, y: 4, z: 8, core: 2. Of those that a mesh axis runs over, the one named last changes fastest.
Arguments:
- position: float32 [3, 262144], P(None, 'src'), may hold values from -3 to 3
- velocity: float32 [3, 262144], P(None, 'src'), may hold values from -3 to 3
- accel: float32 [3, 262144], P(None, 'src'), may hold values from -6 to 6
- jerk_old: float32 [3, 262144], P(None, 'src'), may hold values from -6 to 6
- masses: float32 [262144], P('src'), may hold values from 1.9073486e-06 to 1.5258789e-05
- phase: float32 [262144], P('src'), may hold values from 0.25 to 1
- levels: int32 [262144], P('src'), may hold values from 0 to 3
- active: int32 [16, 128], P('act'), may hold values from 0 to 262143, as said below
Outputs:
- new_position: float32 [3, 262144], P(None, 'src')
- new_velocity: float32 [3, 262144], P(None, 'src')
- new_accel: float32 [3, 262144], P(None, 'src')
- new_jerk: float32 [3, 262144], P(None, 'src')
- active_update: float32 [12, 2048], P(None, 'act')
Inputs may be any that keep to these rules, and one draw needn't show every extreme that they name: The 2048 active indices are distinct star indices. At most 64 active indices fall among the 2048 stars held by one index of src, and exactly 64 do at some index in every draw.
All inputs are finite; a program needn't handle non-finite values.
Results may differ from a plain program's by a relative error of at most 0.0001.
Values sent between devices are 32-bit elements; how exact they have to be, the bound alone decides.
No kernel may reach another device: no remote copies, remote signals or barrier semaphores. Data moves between devices by JAX's collectives and lax.ppermute only.
A program may use at most 64 MiB of HBM per device.

v0:
```python
import math

import jax
import jax.numpy as jnp
from jax import lax
from jax.sharding import PartitionSpec as P

softening = 0.0025


def predict(position, velocity, accel, jerk_old, phase, levels):
    tau = phase * jnp.exp2(-levels.astype(jnp.float32))
    pred_x = position + tau * (velocity + tau * (accel * 0.5 + tau * (jerk_old / 6.0)))
    pred_v = velocity + tau * (accel + tau * (jerk_old * 0.5))
    return (pred_x, pred_v, tau)


def pair_forces(act_x, act_v, src_x, src_v, src_m, width):
    count = src_x.shape[1] // width
    blocks_x = jnp.transpose(src_x.reshape(3, count, width), (1, 0, 2))
    blocks_v = jnp.transpose(src_v.reshape(3, count, width), (1, 0, 2))
    blocks_m = src_m.reshape(count, width)

    def step(carry, item):
        bx, bv, bm = item
        rel_x = bx[:, None, :] - act_x[:, :, None]
        rel_v = bv[:, None, :] - act_v[:, :, None]
        dist = jnp.sum(rel_x * rel_x, axis=0) + softening
        inv = lax.rsqrt(dist)
        weight = bm[None, :] * inv * inv * inv
        radial = 3.0 * jnp.sum(rel_x * rel_v, axis=0) / dist
        acc_add = jnp.sum(weight[None] * rel_x, axis=2)
        jrk_add = jnp.sum(weight[None] * (rel_v - radial[None] * rel_x), axis=2)
        return ((carry[0] + acc_add, carry[1] + jrk_add), None)

    zeros = jnp.zeros(act_x.shape, jnp.float32)
    totals, unused = lax.scan(step, (zeros, zeros), (blocks_x, blocks_v, blocks_m))
    return totals


def correct(state, acc_new, jrk_new):
    pred_x = state[0:3]
    pred_v = state[3:6]
    acc_old = state[6:9]
    jrk_old = state[9:12]
    step_dt = state[12:13]
    delta = acc_old - acc_new
    new_x = pred_x - step_dt * step_dt * (
        0.15 * delta + step_dt * (jrk_old * (7.0 / 60.0) + jrk_new / 30.0)
    )
    new_v = pred_v - step_dt * (0.5 * delta + step_dt * (jrk_old * (5.0 / 12.0) + jrk_new / 12.0))
    return jnp.concatenate([new_x, new_v, acc_new, jrk_new], axis=0)


def local(position, velocity, accel, jerk_old, masses, phase, levels, active):
    local_count = position.shape[1]
    src_index = lax.axis_index("src")
    pred_x, pred_v, tau = predict(position, velocity, accel, jerk_old, phase, levels)
    mine = active.reshape(-1)
    offset = mine - src_index * local_count
    owned = (offset >= 0) & (offset < local_count)
    clipped = jnp.clip(offset, 0, local_count - 1)
    table = jnp.concatenate([pred_x, pred_v, accel, jerk_old, tau[None]], axis=0)
    picked = jnp.take(table, clipped, axis=1) * owned[None].astype(jnp.float32)
    state = lax.psum(picked, "src")
    width = math.gcd(local_count, 256)
    acc_part, jrk_part = pair_forces(state[0:3], state[3:6], pred_x, pred_v, masses, width)
    partial_terms = jnp.concatenate([acc_part, jrk_part], axis=0)
    summed = lax.psum(partial_terms, "src")
    updated = correct(state, summed[0:3], summed[3:6])
    every_update = lax.all_gather(updated, "act", axis=1, tiled=True)
    every_index = lax.all_gather(mine, "act", axis=0, tiled=True)
    target_offset = every_index - src_index * local_count
    target_owned = (target_offset >= 0) & (target_offset < local_count)
    target = jnp.where(target_owned, target_offset, local_count)
    new_position = position.at[:, target].set(every_update[0:3], mode="drop")
    new_velocity = velocity.at[:, target].set(every_update[3:6], mode="drop")
    new_accel = accel.at[:, target].set(every_update[6:9], mode="drop")
    new_jerk = jerk_old.at[:, target].set(every_update[9:12], mode="drop")
    return (new_position, new_velocity, new_accel, new_jerk, updated)


def solution(mesh):
    placed = (
        P(None, "src"),
        P(None, "src"),
        P(None, "src"),
        P(None, "src"),
        P("src"),
        P("src"),
        P("src"),
        P("act", None),
    )
    return jax.shard_map(
        local,
        mesh=mesh,
        in_specs=placed,
        out_specs=(P(None, "src"), P(None, "src"), P(None, "src"), P(None, "src"), P(None, "act")),
        check_vma=False,
    )
```

profile of v0, /device:TPU:1, one launch (start us, length us, event | category | flops | bytes accessed | tf_op | source)
XLA Modules:
  0.0 1443.9 jit_solution(8823686218465949934)
XLA Ops:
  0.6 0.7 broadcast_multiply_fusion
  1.4 0.8 multiply_add_fusion
  2.2 1.7 concatenate.10
  3.9 0.4 copy.114
  4.4 2.8 gather_fusion
  7.4 583.4 %psum.14 = f32[13,1024]{1,0:T(8,128)S(1)} all-reduce(f32[13,1024]{1,0:T(8,128)S(1)} %multiply_bitcast_fusion), channel_id=1, replica_groups=mesh['src'=128,'act'=2] {'src'}, use_global_device_ids=true, to_apply=%region_0.1 | all-reduce | flops 13312 | bytes 106496 | tf_op jit(solution)/shard_map/psum | solution.py:65
  590.9 27.0 %while.13 = (s32[]{:T(128)}, f32[3,1024]{1,0:T(4,128)S(1)}, f32[3,1024]{1,0:T(4,128)S(1)}, f32[8,256]{1,0:T(8,128)S(1)}, f32[8,3,256]{2,1,0:T(4,128)S(1)}, /*ind...) while((s32[]{:T(128)}, f32[3,1024]{1,0:T(4,128)S(1)}, ...), condition=%wide.region_6.7_spmd.clone, body=%wide.region_1.6_spmd.clone.sunk | while | flops 12064771 | bytes 8563835 | solution.py:37
  590.9 1.1 fusion.8
  592.1 0.3 multiply_multiply_fusion.2
  592.3 1.9 fusion.9
  594.3 1.1 fusion.8
  595.4 0.3 multiply_multiply_fusion.2
  595.7 1.9 fusion.9
  597.7 1.1 fusion.8
  598.8 0.3 multiply_multiply_fusion.2
  599.1 1.9 fusion.9
  601.0 1.1 fusion.8
  602.2 0.3 multiply_multiply_fusion.2
  602.5 1.9 fusion.9
  604.4 1.1 fusion.8
  605.6 0.3 multiply_multiply_fusion.2
  605.8 1.9 fusion.9
  607.8 1.1 fusion.8
  608.9 0.3 multiply_multiply_fusion.2
  609.2 1.9 fusion.9
  611.2 1.1 fusion.8
  612.6 1.9 fusion.9
  614.5 1.1 fusion.8
  616.0 1.9 fusion.9
  617.9 572.1 %psum.15 = f32[6,1024]{1,0:T(8,128)S(1)} all-reduce(f32[6,1024]{1,0:T(8,128)S(1)} %pad_maximum_fusion.1), channel_id=1, replica_groups=mesh['src'=128,'act'=2] {'src'}, use_global_device_ids=true, to_apply=%region_7.8 | all-reduce | flops 6144 | bytes 49152 | tf_op jit(solution)/shard_map/psum | solution.py:69
  1190.1 221.1 %all_gather.7 = f32[12,2048]{1,0:T(8,128)S(1)} all-gather(f32[12,1024]{1,0:T(8,128)S(1)} %pad_maximum_fusion), channel_id=1, replica_groups=mesh['src'=128,'act'=2] {'act'}, dimensions={1}, use_global_device_ids=true | all-gather | bytes 147456 | tf_op jit(solution)/shard_map/all_gather | solution.py:71
  1411.2 0.4 copy.121
  1411.6 1.8 all_gather.6
  1413.5 0.4 copy.120
  1413.8 6.0 scatter_fusion.1
  1419.9 0.9 copy.127
  1420.8 0.4 copy.123
  1421.2 0.4 copy.122
  1421.6 6.0 scatter_fusion.2
  1427.6 0.9 copy.128
  1428.5 0.4 copy.125
  1428.9 0.4 copy.124
  1429.3 6.0 scatter_fusion.3
  1435.3 0.9 copy.129
  1436.2 0.4 copy.119
  1436.6 0.4 copy.118
  1437.0 6.0 scatter_fusion
  1443.0 0.9 copy.126
  (65 shorter events, 1.4 us)
Async XLA Ops:
  0.6 3.7 copy-start.5
  4.3 586.5 %copy-start.6 = (f32[2048]{0:T(1024)S(1)}, f32[2048]{0:T(1024)}, u32[]{:S(2)}) copy-start(f32[2048]{0:T(1024)} %param.14) | copy-start | bytes 24580
  617.9 795.6 %copy-start.3 = (f32[3,2048]{1,0:T(4,128)S(1)}, f32[3,2048]{1,0:T(4,128)}, u32[]{:S(2)}) copy-start(f32[3,2048]{1,0:T(4,128)} %param.11) | copy-start | bytes 73732
  1190.1 223.8 %copy-start.2 = (f32[12,1024]{1,0:T(8,128)}, f32[12,1024]{1,0:T(8,128)S(1)}, u32[]{:S(2)}) copy-start(f32[12,1024]{1,0:T(8,128)S(1)} %pad_maximum_fusion) | copy-start | bytes 147460
  1419.9 1.3 copy-start
  1427.6 1.3 copy-start.1
  1435.3 1.3 copy-start.4
where the time goes:
time: 1440 us
  blocking collectives  1380 us (96%)
  local copies, waits for them, and re-layouts  36 us (2%)
  other arithmetic  28 us (2%)
    psum x1, blocking collectives, local(): state = lax.psum(picked, 'src')  583 us
    psum x1, blocking collectives, local(): summed = lax.psum(partial_terms, 'src')  572 us
    all_gather x1, blocking collectives, local(): every_update = lax.all_gather(updated, 'act', axis=1, tiled=True)  221 us

commit v1 on v0

v1 whole, which is shorter than its diff:
```python
import jax
import jax.numpy as jnp
from jax import lax
from jax.experimental import pallas as pl
from jax.experimental.pallas import tpu as pltpu
from jax.sharding import Mesh
from jax.sharding import PartitionSpec as P

softening = 0.0025
SLOTS = 64
LANES = 128
PLANE = ("y", "x")
SRC = ("z", "y", "x")
F32 = jnp.float32
BF16 = jnp.bfloat16
VMEM_LIMIT = 56 * 1024 * 1024


def params():
    return pltpu.CompilerParams(vmem_limit_bytes=VMEM_LIMIT)


def vmem():
    return pl.BlockSpec(memory_space=pltpu.VMEM)


def smem():
    return pl.BlockSpec(memory_space=pltpu.SMEM)


def three_terms(value):
    high = value.astype(BF16)
    rest = value - high.astype(F32)
    middle = rest.astype(BF16)
    low = (rest - middle.astype(F32)).astype(BF16)
    return high, middle, low


def iota(shape, axis):
    return lax.broadcasted_iota(jnp.int32, shape, axis)


def pick_kernel(me_ref, pos_ref, vel_ref, acc_ref, jrk_ref, mass_ref, phase_ref, level_ref, active_ref,
                send_ref, source_ref, place_ref):
    count = pos_ref.shape[1]
    rows = active_ref.shape[0]
    position, velocity = pos_ref[...], vel_ref[...]
    accel, jerk = acc_ref[...], jrk_ref[...]
    tau = phase_ref[...] * jnp.exp2(-level_ref[...].astype(F32))
    pred_x = position + tau * (velocity + tau * (accel * 0.5 + tau * (jerk / 6.0)))
    pred_v = velocity + tau * (accel + tau * (jerk * 0.5))
    base_x = pred_x - tau * tau * (0.15 * accel + tau * (jerk * (7.0 / 60.0)))
    base_v = pred_v - tau * (0.5 * accel + tau * (jerk * (5.0 / 12.0)))
    source_ref[...] = jnp.concatenate([pred_x, pred_v, mass_ref[...], tau], axis=0)

    offset = active_ref[...] - me_ref[0] * count
    owned = (offset >= 0) & (offset < count)
    flag = jnp.where(owned, 1.0, 0.0)
    before = jnp.where(iota((LANES, LANES), 0) < iota((LANES, LANES), 1), 1.0, 0.0)
    inside = jnp.dot(flag.astype(BF16), before.astype(BF16), preferred_element_type=F32)
    totals = jnp.sum(flag, axis=1, keepdims=True)
    running = jnp.zeros((1, 1), F32)
    place = jnp.zeros((SLOTS, LANES), jnp.int32)
    slot_id = iota((SLOTS, LANES), 0)
    for row in range(rows):
        slot = (inside[row:row + 1] + running).astype(jnp.int32)
        slot = jnp.where(owned[row:row + 1], slot, -1)
        place = place + jnp.where(slot_id == slot, offset[row:row + 1] + 1, 0)
        running = running + totals[row:row + 1]
    spot = jnp.sum(place.astype(F32), axis=1, keepdims=True).astype(jnp.int32) - 1
    place_ref[...] = jnp.broadcast_to(spot, (SLOTS, LANES))

    table = jnp.concatenate([pred_x, pred_v, tau, tau, base_x, base_v, tau, tau], axis=0)
    onehot = jnp.where(iota((SLOTS, count), 1) == spot, 1.0, 0.0).astype(BF16)
    picked = jnp.zeros((16, SLOTS), F32)
    for term in three_terms(table):
        picked = picked + lax.dot_general(term, onehot, (((1,), (1,)), ((), ())), preferred_element_type=F32)
    block = jnp.concatenate([picked[0:8], picked[8:16]], axis=1)
    send_ref[...] = jnp.broadcast_to(block[None], send_ref.shape)


def pick(me, position, velocity, accel, jerk_old, masses, phase, levels, active, owners):
    count = position.shape[1]
    return pl.pallas_call(
        pick_kernel,
        out_shape=(
            jax.ShapeDtypeStruct((owners, 8, LANES), F32),
            jax.ShapeDtypeStruct((8, count), F32),
            jax.ShapeDtypeStruct((SLOTS, LANES), jnp.int32),
        ),
        in_specs=[smem()] + [vmem()] * 8,
        out_specs=(vmem(), vmem(), vmem()),
        compiler_params=params(),
        name="pick",
    )(me, position, velocity, accel, jerk_old, masses, phase, levels, active)


def order_kernel(owners, source_ref, active_ref, mine_ref, other_ref, first_ref, perm_ref, onehot_ref, spread_ref):
    count = source_ref.shape[1]
    rows = active_ref.shape[0]
    total = rows * LANES
    active = active_ref[...]
    owner = lax.shift_right_logical(active, count.bit_length() - 1)
    key = (owner * total + iota((rows, LANES), 0) * LANES + iota((rows, LANES), 1)).astype(F32)
    columns = jnp.transpose(key)
    limit = (iota((1, LANES), 1) * total).astype(F32)
    first = jnp.zeros((8, LANES), F32)
    ranks = [jnp.zeros((8, LANES), F32) for _ in range(rows)]
    for row in range(rows):
        column = jnp.broadcast_to(columns[:, row:row + 1], (LANES, LANES))
        first = first + jnp.sum(jnp.where(column < limit, 1.0, 0.0).reshape(LANES // 8, 8, LANES), axis=0)
        for to in range(rows):
            less = jnp.where(column < key[to:to + 1], 1.0, 0.0)
            ranks[to] = ranks[to] + jnp.sum(less.reshape(LANES // 8, 8, LANES), axis=0)
    first_ref[...] = jnp.sum(first, axis=0, keepdims=True).astype(jnp.int32)
    spots = iota((total, LANES), 0)
    for to in range(rows):
        rank = jnp.sum(ranks[to], axis=0, keepdims=True).astype(jnp.int32)
        perm_ref[:, to * LANES:(to + 1) * LANES] = jnp.where(spots == rank, 1.0, 0.0).astype(BF16)
    lanes = iota((SLOTS, LANES), 1)
    for piece in range(count // LANES):
        here = slice(piece * LANES, (piece + 1) * LANES)
        onehot_ref[0:SLOTS, here] = jnp.where(mine_ref[...] == lanes + piece * LANES, 1.0, 0.0).astype(BF16)
        onehot_ref[SLOTS:2 * SLOTS, here] = jnp.where(other_ref[...] == lanes + piece * LANES, 1.0, 0.0).astype(BF16)
        across = jnp.transpose(source_ref[:, here])
        for field in range(7):
            spread_ref[field, here, :] = jnp.broadcast_to(across[:, field:field + 1], (LANES, LANES))


def order(source, active, mine, other, owners):
    count = source.shape[1]
    total = active.shape[0] * LANES
    return pl.pallas_call(
        lambda *refs: order_kernel(owners, *refs),
        out_shape=(
            jax.ShapeDtypeStruct((1, LANES), jnp.int32),
            jax.ShapeDtypeStruct((total, total), BF16),
            jax.ShapeDtypeStruct((2 * SLOTS, count), BF16),
            jax.ShapeDtypeStruct((7, count, LANES), F32),
        ),
        in_specs=[vmem()] * 4,
        out_specs=(vmem(), vmem(), vmem(), vmem()),
        compiler_params=params(),
        name="order",
    )(source, active, mine, other)


def force_kernel(first_ref, states_ref, spread_ref, send_ref, state_ref, compact):
    owners = states_ref.shape[0]
    count = spread_ref.shape[1]
    blocks = state_ref.shape[1]
    lane = iota((8, LANES), 1)

    def place(owner, unused):
        start = first_ref[0, owner]
        block = lax.shift_right_logical(start, 7)
        shift = lax.bitwise_and(start, LANES - 1)
        value = states_ref[owner]
        keep = lane >= shift
        for half in range(2):
            turned = pltpu.roll(value, lax.bitwise_and(shift + half * SLOTS, LANES - 1), 1)
            pltpu.store(compact.at[half, block], turned, mask=keep)
            compact[half, block + 1] = turned
        return unused

    lax.fori_loop(0, owners, place, 0, unroll=8)
    for field in range(16):
        state_ref[field] = compact[field // 8, 0:blocks, field % 8, :]

    width = 2
    for block in range(0, blocks, width):
        stars = [[jnp.broadcast_to(compact[0, block + b, f:f + 1, :], (8, LANES)) for f in range(6)] for b in range(width)]

        def step(group, sums):
            here = pl.ds(pl.multiple_of(group * 8, 8), 8)
            source = [spread_ref[f, here, :] for f in range(7)]
            result = []
            for b in range(width):
                star = stars[b]
                rx = [source[d] - star[d] for d in range(3)]
                rv = [source[3 + d] - star[3 + d] for d in range(3)]
                dist = rx[0] * rx[0] + rx[1] * rx[1] + (rx[2] * rx[2] + softening)
                inv = lax.rsqrt(dist)
                inv2 = inv * inv
                weight = source[6] * inv * inv2
                dot = rx[0] * rv[0] + rx[1] * rv[1] + rx[2] * rv[2]
                radial = weight * inv2 * dot
                old = sums[b]
                result.append(
                    tuple(old[d] + weight * rx[d] for d in range(3))
                    + tuple(old[3 + d] + weight * rv[d] for d in range(3))
                    + tuple(old[6 + d] + radial * rx[d] for d in range(3))
                )
            return tuple(result)

        zero = jnp.zeros((8, LANES), F32)
        sums = lax.fori_loop(0, count // 8, step, tuple((zero,) * 9 for _ in range(width)), unroll=2)
        for b in range(width):
            for d in range(3):
                acc = jnp.sum(sums[b][d], axis=0, keepdims=True)
                jrk = jnp.sum(sums[b][3 + d] - 3.0 * sums[b][6 + d], axis=0, keepdims=True)
                row = d * blocks + block + b
                send_ref[0, row:row + 1, :] = acc
                row = row + 3 * blocks
                send_ref[0, row:row + 1, :] = jrk
    for peer in range(1, send_ref.shape[0]):
        send_ref[peer] = send_ref[0]


def forces(first, states, spread, blocks, peers):
    return pl.pallas_call(
        force_kernel,
        out_shape=(
            jax.ShapeDtypeStruct((peers, 6 * blocks, LANES), F32),
            jax.ShapeDtypeStruct((16, blocks, LANES), F32),
        ),
        in_specs=[smem(), vmem(), vmem()],
        out_specs=(vmem(), vmem()),
        scratch_shapes=[pltpu.VMEM((2, blocks + 2, 8, LANES), F32)],
        compiler_params=params(),
        name="forces",
    )(first, states, spread)


def add_kernel(parts_ref, send_ref):
    total = jnp.sum(parts_ref[...], axis=0)
    send_ref[...] = jnp.broadcast_to(total[None], send_ref.shape)


def add_parts(parts, peers):
    return pl.pallas_call(
        add_kernel,
        out_shape=jax.ShapeDtypeStruct((peers,) + parts.shape[1:], F32),
        in_specs=[vmem()],
        out_specs=vmem(),
        compiler_params=params(),
        name="add_parts",
    )(parts)


def correct_kernel(me_ref, first_ref, parts_ref, state_ref, perm_ref, update_ref, own_ref, wide):
    blocks = state_ref.shape[1]
    total = jnp.sum(parts_ref[...], axis=0)
    tau = state_ref[6]
    t2 = tau * tau
    for d in range(3):
        acc = total[d * blocks:(d + 1) * blocks]
        jrk = total[(3 + d) * blocks:(4 + d) * blocks]
        wide[d, 0:blocks] = state_ref[8 + d] + t2 * (0.15 * acc - tau * (jrk / 30.0))
        wide[3 + d, 0:blocks] = state_ref[11 + d] + tau * (0.5 * acc - tau * (jrk / 12.0))
        wide[6 + d, 0:blocks] = acc
        wide[9 + d, 0:blocks] = jrk
    for f in range(12, 16):
        wide[f, 0:blocks] = jnp.ones_like(tau)
    wide[:, blocks:] = jnp.zeros((16, wide.shape[1] - blocks, LANES), F32)
    result = jnp.zeros((16, blocks * LANES), F32)
    for block in range(blocks):
        part = wide[:, block, :]
        rows = perm_ref[block * LANES:(block + 1) * LANES, :]
        for term in three_terms(part):
            result = result + jnp.dot(term, rows, preferred_element_type=F32)
    update_ref[...] = result[0:12]

    start = first_ref[0, me_ref[0]]
    block = lax.shift_right_logical(start, 7)
    shift = lax.bitwise_and(start, LANES - 1)
    back = lax.bitwise_and(LANES - shift, LANES - 1)
    lane = iota((16, LANES), 1)
    low = pltpu.roll(wide[:, block, :], back, 1)
    high = pltpu.roll(wide[:, block + 1, :], back, 1)
    own_ref[...] = jnp.where(lane < LANES - shift, low, high)


def correct(me, first, parts, state, perm):
    blocks = state.shape[1]
    return pl.pallas_call(
        correct_kernel,
        out_shape=(
            jax.ShapeDtypeStruct((12, blocks * LANES), F32),
            jax.ShapeDtypeStruct((16, LANES), F32),
        ),
        in_specs=[smem(), smem(), vmem(), vmem(), vmem()],
        out_specs=(vmem(), vmem()),
        scratch_shapes=[pltpu.VMEM((16, blocks + 2, LANES), F32)],
        compiler_params=params(),
        name="correct",
    )(me, first, parts, state, perm)


def write_kernel(mine_ref, other_ref, onehot_ref, pos_ref, vel_ref, acc_ref, jrk_ref,
                 new_pos_ref, new_vel_ref, new_acc_ref, new_jrk_ref):
    both = jnp.concatenate([mine_ref[:, 0:SLOTS], other_ref[:, 0:SLOTS]], axis=1)
    onehot = onehot_ref[...]
    values = jnp.zeros((16, onehot.shape[1]), F32)
    for term in three_terms(both):
        values = values + jnp.dot(term, onehot, preferred_element_type=F32)
    hit = values[12:13] > 0.5
    new_pos_ref[...] = jnp.where(hit, values[0:3], pos_ref[...])
    new_vel_ref[...] = jnp.where(hit, values[3:6], vel_ref[...])
    new_acc_ref[...] = jnp.where(hit, values[6:9], acc_ref[...])
    new_jrk_ref[...] = jnp.where(hit, values[9:12], jrk_ref[...])


def write(mine, other, onehot, position, velocity, accel, jerk_old):
    shape = jax.ShapeDtypeStruct(position.shape, F32)
    return pl.pallas_call(
        write_kernel,
        out_shape=(shape,) * 4,
        in_specs=[vmem()] * 7,
        out_specs=(vmem(),) * 4,
        compiler_params=params(),
        name="write",
    )(mine, other, onehot, position, velocity, accel, jerk_old)


def swap(value):
    return lax.ppermute(value, "core", [(0, 1), (1, 0)])


def exchange(value, axes):
    return lax.all_to_all(value, axes, 0, 0, tiled=True)


def local(owners, plane, depth, position, velocity, accel, jerk_old, masses, phase, levels, active):
    count = position.shape[1]
    blocks = active.shape[0]
    me = lax.axis_index(SRC).reshape(1).astype(jnp.int32)
    send, source, mine = pick(
        me, position, velocity, accel, jerk_old, masses.reshape(1, count), phase.reshape(1, count),
        levels.reshape(1, count), active, owners,
    )
    states = exchange(send, SRC)
    other = swap(mine)
    first, perm, onehot, spread = order(source, active, mine, other, owners)
    send, state = forces(first, states, spread, blocks, plane)
    send = add_parts(exchange(send, PLANE), depth)
    update, own = correct(me, first, exchange(send, "z"), state, perm)
    new = write(own, swap(own), onehot, position, velocity, accel, jerk_old)
    return new + (update,)


def solution(mesh):
    owners = mesh.shape["src"]
    plane = 16
    depth = owners // plane
    fine = Mesh(mesh.devices.reshape(depth, 4, 4, mesh.shape["act"]), ("z", "y", "x", "core"))
    stars = P(None, SRC)
    placed = (stars,) * 4 + (P(SRC),) * 3 + (P("core", None),)
    return jax.shard_map(
        lambda *arrays: local(owners, plane, depth, *arrays),
        mesh=fine,
        in_specs=placed,
        out_specs=(stars,) * 4 + (P(None, "core"),),
        check_vma=False,
    )
```

time: 1440 us -> 100 us (0.07)
  blocking collectives: 1380 us -> 25.3 us
  Pallas kernels: 0 us -> 39.3 us
  local copies, waits for them, and re-layouts: 36 us -> 2 us
  other arithmetic: 28 us -> 0 us
  starting transfers between devices: 0 us -> 22.8 us
    psum x2 -> x0, blocking collectives: 1160 us -> none  [the longest x1 583 us: local(): state = lax.psum(picked, 'src')]
    all_gather x2 -> x0, blocking collectives: 223 us -> none  [the longest x1 221 us: local(): every_update = lax.all_gather(updated, 'act', axis=1, tiled=True)]
    pallas_call x0 -> x6, Pallas kernels: none -> 39.3 us  [the longest x1 21.4 us: forces(): pl.pallas_call(force_kernel, out_shape=(jax.ShapeDtypeStruct((peers, 6 *...]
    all_to_all x0 -> x2, blocking collectives: none -> 25.3 us  [exchange(): return lax.all_to_all(value, axes, 0, 0, tiled=True)]
    scatter x4 -> x0, local copies, waits for them, and re-layouts: 24 us -> none  [the longest x1 6 us: local(): new_velocity = velocity.at[:, target].set(every_update[3:6], mode='drop')]
    reduce_sum x16 -> x0, other arithmetic: 23.8 us -> none  [the longest x8 14.9 us: step(): jrk_add = jnp.sum(weight[None] * (rel_v - radial[None] * rel_x), axis=2)]
    all_to_all x0 -> x1, starting transfers between devices: none -> 16.3 us  [exchange(): return lax.all_to_all(value, axes, 0, 0, tiled=True)]
  transfers between devices with their start and end apart: 0 -> 3, of which waited for: 0 -> 3; matrix products, arithmetic and copies ran while one was open for 0% -> 0% of each run, Pallas kernels for 0% -> 8%
where the time goes in v1:
time: 100 us; the launch traced here: 99.4 us
  Pallas kernels  39.3 us (39%)
  blocking collectives  25.3 us (25%)
  starting transfers between devices  22.8 us (23%)
  waiting for transfers between devices  9.4 us (9%)
  local copies, waits for them, and re-layouts  2 us (2%)
    all_to_all x2, blocking collectives, exchange(): return lax.all_to_all(value, axes, 0, 0, tiled=True)  25.3 us
    pallas_call x1, Pallas kernels, forces(): pl.pallas_call(force_kernel, out_shape=(jax.ShapeDtypeStruct((peers, 6 *...  21.4 us
    all_to_all x1, starting transfers between devices, exchange(): return lax.all_to_all(value, axes, 0, 0, tiled=True)  16.3 us
    pallas_call x1, Pallas kernels, order(): pl.pallas_call(lambda *refs: order_kernel(owners, *refs), out_shape=(jax....  8.27 us
    all_to_all x1, waiting for transfers between devices, exchange(): return lax.all_to_all(value, axes, 0, 0, tiled=True)  7.29 us
    ppermute x2, starting transfers between devices, swap(): return lax.ppermute(value, 'core', [(0, 1), (1, 0)])  6.45 us
    pallas_call x1, Pallas kernels, correct(): pl.pallas_call(correct_kernel, out_shape=(jax.ShapeDtypeStruct((12, block...  3.34 us
    pallas_call x1, Pallas kernels, pick(): pl.pallas_call(pick_kernel, out_shape=(jax.ShapeDtypeStruct((owners, 8, L...  2.37 us
  transfers between devices with their start and end apart: 3, of which 3 were waited for; matrix products, arithmetic and copies ran while one was open for 0% of the time, Pallas kernels for 8%

profile of v1, /device:TPU:1, one launch (start us, length us, event | category | flops | bytes accessed | tf_op | source)
XLA Modules:
  0.0 99.4 jit_solution(3942803990976093732)
XLA Ops:
  0.6 2.4 %pick.1 = (f32[128,8,128]{2,1,0:T(8,128)}, f32[8,2048]{1,0:T(8,128)}, s32[64,128]{1,0:T(8,128)}) custom-call(s32[1]{0:T(128)} %bitcast.me_ref, f32[3,2048]{1,0:T(4,128)} %pos_ref.3, f32[3,2048]{1,0:T(4,128)} %vel_ref.3, f32[3,2048]{1,0:T(4,128)} %acc_ref.3, f32[3,2048]{1,0:T(4,128)} %jrk_ref.3, f32[1,2048]{1,0:T(1,128)} %bitcast.4, f32[1,2048]{1,0:T(1,128)} %bitcast.5, ...), custom_call_target="tpu_custom_call" | custom-call | tf_op jit(solution)/shard_map/pick/pallas_call | solution.py:84
  3.0 16.3 %all-to-all-start = ((f32[128,8,128]{2,1,0:T(8,128)}), f32[128,8,128]{2,1,0:T(8,128)S(1)}, u32[]{:S(2)}, u32[]{:S(2)}) async-start(f32[128,8,128]{2,1,0:T(8,128)} %get-tuple-element.23), calls=%async_computation | async-start | bytes 1048576 | tf_op jit(solution)/shard_map/all_to_all | solution.py:321
  19.4 1.0 %collective-permute-start = (s32[64,128]{1,0:T(8,128)}, s32[64,128]{1,0:T(8,128)S(1)}, u32[]{:S(2)}, u32[]{:S(2)}) collective-permute-start(s32[64,128]{1,0:T(8,128)} %get-tuple-element.21.refs_2_), channel_id=1, source_target_pairs={{0,1},{1,0},{2,3},{3,2},{4,5},{5,4},{6,7},{7,6},{8,9},{9,8},{10,11... | collective-permute-start | bytes 98312 | tf_op jit(solution)/shard_map/ppermute | solution.py:317
  20.4 1.1 %collective-permute-done.refs_3_ = s32[64,128]{1,0:T(8,128)S(1)} collective-permute-done((s32[64,128]{1,0:T(8,128)}, s32[64,128]{1,0:T(8,128)S(1)}, u32[]{:S(2)}, u32[]{:S(2)}) %collective-permute-start) | collective-permute-done | bytes 32800 | tf_op jit(solution)/shard_map/ppermute | solution.py:317
  21.5 0.0 copy-start.1
  21.5 0.6 copy-done.1
  22.1 8.3 %order.1 = (s32[1,128]{1,0:T(1,128)}, bf16[1024,1024]{1,0:T(8,128)(2,1)}, bf16[128,2048]{1,0:T(8,128)(2,1)}, f32[7,2048,128]{2,1,0:T(8,128)}) custom-call(f32[8,2048]{1,0:T(8,128)} %get-tuple-element.20.refs_0_, s32[8,128]{1,0:T(8,128)} %refs_1_.1, s32[64,128]{1,0:T(8,128)} %get-tuple-element.21.refs_2_, s32[64,128]{1,0:T(8,128)} %copy-done.1), custom_call_target="tpu_custom_call" | custom-call | tf_op jit(solution)/shard_map/order/pallas_call | solution.py:133
  30.4 7.3 %all-to-all-done.states_ref = f32[128,8,128]{2,1,0:T(8,128)S(1)} async-done(((f32[128,8,128]{2,1,0:T(8,128)}), f32[128,8,128]{2,1,0:T(8,128)S(1)}, u32[]{:S(2)}, u32[]{:S(2)}) %all-to-all-start) | async-done | bytes 524320 | tf_op jit(solution)/shard_map/all_to_all | solution.py:321
  37.7 0.0 copy-start
  37.7 0.8 copy-done
  38.4 21.4 %forces.1 = (f32[16,48,128]{2,1,0:T(8,128)}, f32[16,8,128]{2,1,0:T(8,128)}) custom-call(s32[1,128]{1,0:T(1,128)} %get-tuple-element.22.first_ref, f32[128,8,128]{2,1,0:T(8,128)} %copy-done, f32[7,2048,128]{2,1,0:T(8,128)} %get-tuple-element.24.spread_ref), custom_call_target="tpu_custom_call" | custom-call | tf_op jit(solution)/shard_map/forces/pallas_call | solution.py:211
  59.9 12.7 %all_to_all.15.parts_ref = f32[16,48,128]{2,1,0:T(8,128)} all-to-all(f32[16,48,128]{2,1,0:T(8,128)} %get-tuple-element.25), channel_id=1, replica_groups=mesh['z'=8,'y'=4,'x'=4,'core'=2] {'y','x'}, dimensions={0} | all-to-all | bytes 786432 | tf_op jit(solution)/shard_map/all_to_all | solution.py:321
  72.5 1.7 %add_parts.1 = f32[8,48,128]{2,1,0:T(8,128)} custom-call(f32[16,48,128]{2,1,0:T(8,128)} %all_to_all.15.parts_ref), custom_call_target="tpu_custom_call" | custom-call | tf_op jit(solution)/shard_map/add_parts/pallas_call | solution.py:231
  74.2 12.6 %all_to_all.16.parts_ref = f32[8,48,128]{2,1,0:T(8,128)} all-to-all(f32[8,48,128]{2,1,0:T(8,128)} %add_parts.1), channel_id=1, replica_groups=mesh['z'=8,'y'=4,'x'=4,'core'=2] {'z'}, dimensions={0} | all-to-all | bytes 393216 | tf_op jit(solution)/shard_map/all_to_all | solution.py:321
  86.9 3.3 %correct.1 = (f32[12,1024]{1,0:T(8,128)}, f32[16,128]{1,0:T(8,128)}) custom-call(s32[1]{0:T(128)} %bitcast.me_ref, s32[1,128]{1,0:T(1,128)} %get-tuple-element.22.first_ref, f32[8,48,128]{2,1,0:T(8,128)} %all_to_all.16.parts_ref, f32[16,8,128]{2,1,0:T(8,128)} %get-tuple-element.26.state_ref, bf16[1024,1024]{1,0:T(8,128)(2,1)} %get-tuple-element.27.perm_ref), custom_call_target="tpu_custom_call" | custom-call | tf_op jit(solution)/shard_map/correct/pallas_call | solution.py:276
  90.2 5.4 %collective-permute-start.1 = (f32[16,128]{1,0:T(8,128)}, f32[16,128]{1,0:T(8,128)S(1)}, u32[]{:S(2)}, u32[]{:S(2)}) collective-permute-start(f32[16,128]{1,0:T(8,128)} %get-tuple-element.28.mine_ref), channel_id=1, source_target_pairs={{0,1},{1,0},{2,3},{3,2},{4,5},{5,4},{6,7},{7,6},{8,9},{9,8},{10,11... | collective-permute-start | bytes 24584 | tf_op jit(solution)/shard_map/ppermute | solution.py:317
  95.6 1.0 %collective-permute-done.1.other_ref = f32[16,128]{1,0:T(8,128)S(1)} collective-permute-done((f32[16,128]{1,0:T(8,128)}, f32[16,128]{1,0:T(8,128)S(1)}, u32[]{:S(2)}, u32[]{:S(2)}) %collective-permute-start.1) | collective-permute-done | bytes 8224 | tf_op jit(solution)/shard_map/ppermute | solution.py:317
  96.7 0.0 copy-start.2
  96.7 0.6 copy-done.2
  97.2 2.1 %write.1 = (f32[3,2048]{1,0:T(4,128)}, f32[3,2048]{1,0:T(4,128)}, f32[3,2048]{1,0:T(4,128)}, f32[3,2048]{1,0:T(4,128)}) custom-call(f32[16,128]{1,0:T(8,128)} %get-tuple-element.28.mine_ref, f32[16,128]{1,0:T(8,128)} %copy-done.2, bf16[128,2048]{1,0:T(8,128)(2,1)} %get-tuple-element.29.onehot_ref, f32[3,2048]{1,0:T(4,128)} %pos_ref.3, f32[3,2048]{1,0:T(4,128)} %vel_ref.3, ...), custom_call_target="tpu_custom_call" | custom-call | tf_op jit(solution)/shard_map/write/pallas_call | solution.py:306
Async XLA Ops:
  3.0 34.6 %all-to-all-start = ((f32[128,8,128]{2,1,0:T(8,128)}), f32[128,8,128]{2,1,0:T(8,128)S(1)}, u32[]{:S(2)}, u32[]{:S(2)}) async-start(f32[128,8,128]{2,1,0:T(8,128)} %get-tuple-element.23), calls=%async_computation | async-start | bytes 1048576 | tf_op jit(solution)/shard_map/all_to_all | solution.py:321
  19.4 2.1 %collective-permute-start = (s32[64,128]{1,0:T(8,128)}, s32[64,128]{1,0:T(8,128)S(1)}, u32[]{:S(2)}, u32[]{:S(2)}) collective-permute-start(s32[64,128]{1,0:T(8,128)} %get-tuple-element.21.refs_2_), channel_id=1, source_target_pairs={{0,1},{1,0},{2,3},{3,2},{4,5},{5,4},{6,7},{7,6},{8,9},{9,8},{10,11... | collective-permute-start | bytes 98312 | tf_op jit(solution)/shard_map/ppermute | solution.py:317
  21.5 0.6 copy-start.1
  37.7 0.8 copy-start
  90.2 6.4 %collective-permute-start.1 = (f32[16,128]{1,0:T(8,128)}, f32[16,128]{1,0:T(8,128)S(1)}, u32[]{:S(2)}, u32[]{:S(2)}) collective-permute-start(f32[16,128]{1,0:T(8,128)} %get-tuple-element.28.mine_ref), channel_id=1, source_target_pairs={{0,1},{1,0},{2,3},{3,2},{4,5},{5,4},{6,7},{7,6},{8,9},{9,8},{10,11... | collective-permute-start | bytes 24584 | tf_op jit(solution)/shard_map/ppermute | solution.py:317
  96.7 0.6 copy-start.2

commit v2 on v1

v2 whole, which is shorter than its diff:
```python
import jax
import jax.numpy as jnp
from jax import lax
from jax.experimental import pallas as pl
from jax.experimental.pallas import tpu as pltpu
from jax.sharding import Mesh
from jax.sharding import PartitionSpec as P

softening = 0.0025
SLOTS = 64
LANES = 128
PLANE = ("y", "x")
SRC = ("z", "y", "x")
F32 = jnp.float32
BF16 = jnp.bfloat16
PREP = 56
PAIRS = ((0, 0), (0, 1), (1, 0), (1, 1), (0, 2), (2, 0))


def params(mebibytes):
    return pltpu.CompilerParams(vmem_limit_bytes=mebibytes << 20)


def cost(microseconds):
    return pl.CostEstimate(flops=0, transcendentals=0, bytes_accessed=microseconds * 3000000)


def vmem():
    return pl.BlockSpec(memory_space=pltpu.VMEM)


def hbm():
    return pl.BlockSpec(memory_space=pltpu.HBM)


def pinned(value):
    return pltpu.with_memory_space_constraint(value, pltpu.HBM)


def smem():
    return pl.BlockSpec(memory_space=pltpu.SMEM)


def three_terms(value):
    high = value.astype(BF16)
    rest = value - high.astype(F32)
    middle = rest.astype(BF16)
    low = (rest - middle.astype(F32)).astype(BF16)
    return high, middle, low


def iota(shape, axis):
    return lax.broadcasted_iota(jnp.int32, shape, axis)


def pick_kernel(me_ref, pos_ref, vel_ref, acc_ref, jrk_ref, mass_ref, phase_ref, level_ref, active_ref,
                send_ref, source_ref, place_ref):
    count = pos_ref.shape[1]
    rows = active_ref.shape[0]
    position, velocity = pos_ref[...], vel_ref[...]
    accel, jerk = acc_ref[...], jrk_ref[...]
    tau = phase_ref[...] * jnp.exp2(-level_ref[...].astype(F32))
    pred_x = position + tau * (velocity + tau * (accel * 0.5 + tau * (jerk / 6.0)))
    pred_v = velocity + tau * (accel + tau * (jerk * 0.5))
    base_x = pred_x - tau * tau * (0.15 * accel + tau * (jerk * (7.0 / 60.0)))
    base_v = pred_v - tau * (0.5 * accel + tau * (jerk * (5.0 / 12.0)))
    source_ref[...] = jnp.concatenate([pred_x, pred_v, mass_ref[...], tau], axis=0)

    offset = active_ref[...] - me_ref[0] * count
    owned = (offset >= 0) & (offset < count)
    flag = jnp.where(owned, 1.0, 0.0)
    before = jnp.where(iota((LANES, LANES), 0) < iota((LANES, LANES), 1), 1.0, 0.0)
    inside = jnp.dot(flag.astype(BF16), before.astype(BF16), preferred_element_type=F32)
    totals = jnp.sum(flag, axis=1, keepdims=True)
    running = jnp.zeros((1, 1), F32)
    place = jnp.zeros((SLOTS, LANES), jnp.int32)
    slot_id = iota((SLOTS, LANES), 0)
    for row in range(rows):
        slot = (inside[row:row + 1] + running).astype(jnp.int32)
        slot = jnp.where(owned[row:row + 1], slot, -1)
        place = place + jnp.where(slot_id == slot, offset[row:row + 1] + 1, 0)
        running = running + totals[row:row + 1]
    spot = jnp.sum(place.astype(F32), axis=1, keepdims=True).astype(jnp.int32) - 1
    place_ref[...] = jnp.broadcast_to(spot, (SLOTS, LANES))

    table = jnp.concatenate([pred_x, pred_v, tau, tau, base_x, base_v, tau, tau], axis=0)
    onehot = jnp.where(iota((SLOTS, count), 1) == spot, 1.0, 0.0).astype(BF16)
    terms = jnp.concatenate(three_terms(table), axis=0)
    picked = lax.dot_general(terms, onehot, (((1,), (1,)), ((), ())), preferred_element_type=F32)
    picked = picked[0:16] + picked[16:32] + picked[32:48]
    block = jnp.concatenate([picked[0:8], picked[8:16]], axis=1)
    send_ref[...] = jnp.broadcast_to(block[None], send_ref.shape)


def pick(me, position, velocity, accel, jerk_old, masses, phase, levels, active, owners):
    count = position.shape[1]
    return pl.pallas_call(
        pick_kernel,
        out_shape=(
            jax.ShapeDtypeStruct((owners, 8, LANES), F32),
            jax.ShapeDtypeStruct((8, count), F32),
            jax.ShapeDtypeStruct((SLOTS, LANES), jnp.int32),
        ),
        in_specs=[smem()] + [vmem()] * 8,
        out_specs=(vmem(), vmem(), vmem()),
        compiler_params=params(56),
        name="pick",
    )(me, position, velocity, accel, jerk_old, masses, phase, levels, active)


def sort_keys(active, count):
    rows = active.shape[0]
    owner = lax.shift_right_logical(active, count.bit_length() - 1)
    return (owner * (rows * LANES) + iota((rows, LANES), 0) * LANES + iota((rows, LANES), 1)).astype(F32)


def prepare_kernel(source_ref, active_ref, first_ref, factor_ref, moment_ref, spread_ref):
    count = source_ref.shape[1]
    rows = active_ref.shape[0]
    total = rows * LANES
    key = sort_keys(active_ref[...], count)
    columns = jnp.transpose(key)
    limit = (iota((1, LANES), 1) * total).astype(F32)
    first = jnp.zeros((8, LANES), F32)
    for row in range(rows):
        column = jnp.broadcast_to(columns[:, row:row + 1], (LANES, LANES))
        first = first + jnp.sum(jnp.where(column < limit, 1.0, 0.0).reshape(LANES // 8, 8, LANES), axis=0)
    first_ref[...] = jnp.sum(first, axis=0, keepdims=True).astype(jnp.int32)

    source = source_ref[...]
    terms = [term.astype(F32) for term in three_terms(source)]
    product = source[0:1] * source[3:4] + source[1:2] * source[4:5] + source[2:3] * source[5:6]
    product = [term.astype(F32) for term in three_terms(product)]
    one = jnp.ones((3, count), F32)
    last = jnp.concatenate(product + [one, jnp.zeros((2, count), F32)], axis=0)
    stack = jnp.concatenate([terms[a] for a, unused in PAIRS] + [last], axis=0)
    mass = source[6:7]
    moments = jnp.concatenate([mass * source[0:6], mass, jnp.zeros((1, count), F32)], axis=0)
    moments = [term.astype(F32) for term in three_terms(moments)]
    moment_ref[...] = jnp.concatenate(moments + [jnp.zeros((8, count), F32)], axis=0).astype(BF16)
    for piece in range(count // LANES):
        here = slice(piece * LANES, (piece + 1) * LANES)
        across = jnp.transpose(stack[:, here])
        factor_ref[here, :] = jnp.concatenate([across, jnp.zeros((LANES, LANES - 56), F32)], axis=1).astype(BF16)
        across = jnp.transpose(source[:, here])
        for field in range(3):
            spread_ref[field, here, :] = jnp.broadcast_to(across[:, field:field + 1], (LANES, LANES))


def prepare(source, active):
    count = source.shape[1]
    return pl.pallas_call(
        prepare_kernel,
        out_shape=(
            jax.ShapeDtypeStruct((1, LANES), jnp.int32),
            jax.ShapeDtypeStruct((count, LANES), BF16),
            jax.ShapeDtypeStruct((32, count), BF16),
            jax.ShapeDtypeStruct((3, count, LANES), F32),
        ),
        in_specs=[vmem()] * 2,
        out_specs=(vmem(),) * 4,
        compiler_params=params(PREP),
        cost_estimate=cost(5),
        name="prepare",
    )(source, active)


def place(first_ref, states_ref, compact, half, owner):
    start = first_ref[0, owner]
    block = lax.shift_right_logical(start, 7)
    shift = lax.bitwise_and(start, LANES - 1)
    turned = pltpu.roll(states_ref[owner], lax.bitwise_and(shift + half * SLOTS, LANES - 1), 1)
    pltpu.store(compact.at[block], turned, mask=iota((8, LANES), 1) >= shift)
    compact[block + 1] = turned


def tables_kernel(count, active_ref, perm_ref):
    rows = active_ref.shape[0]
    total = rows * LANES
    key = sort_keys(active_ref[...], count)
    columns = jnp.transpose(key)
    ranks = [jnp.zeros((8, LANES), F32) for _ in range(rows)]
    for row in range(rows):
        column = jnp.broadcast_to(columns[:, row:row + 1], (LANES, LANES))
        for to in range(rows):
            less = jnp.where(column < key[to:to + 1], 1.0, 0.0)
            ranks[to] = ranks[to] + jnp.sum(less.reshape(LANES // 8, 8, LANES), axis=0)
    spots = iota((total, LANES), 0)
    for to in range(rows):
        rank = jnp.sum(ranks[to], axis=0, keepdims=True).astype(jnp.int32)
        perm_ref[:, to * LANES:(to + 1) * LANES] = jnp.where(spots == rank, 1.0, 0.0).astype(BF16)


def tables(active, count):
    total = active.shape[0] * LANES
    return pl.pallas_call(
        lambda *refs: tables_kernel(count, *refs),
        out_shape=jax.ShapeDtypeStruct((total, total), BF16),
        in_specs=[vmem()],
        out_specs=vmem(),
        compiler_params=params(8),
        cost_estimate=cost(4),
        name="tables",
    )(active)


def force_kernel(first_hbm, states_ref, factor_hbm, moment_hbm, spread_hbm, send_ref, state_ref,
                 compact, later, first_ref, factor_ref, moment_ref, spread_ref, arrived):
    owners = states_ref.shape[0]
    count = spread_ref.shape[1]
    blocks = send_ref.shape[1] // 6
    pairs = ((first_hbm, first_ref), (factor_hbm, factor_ref), (moment_hbm, moment_ref), (spread_hbm, spread_ref))
    copies = [pltpu.make_async_copy(here, there, arrived.at[i]) for i, (here, there) in enumerate(pairs)]
    for copy in copies:
        copy.start()
    copies[0].wait()

    def place_early(owner, unused):
        place(first_ref, states_ref, compact, 0, owner)
        return unused

    lax.fori_loop(0, owners, place_early, 0, unroll=16)
    for copy in copies[1:]:
        copy.wait()
    wide, deep = 2, min(1024, count)
    width = wide * LANES

    def part(block):
        tiles = [compact[block + b] for b in range(wide)]
        star = jnp.concatenate(tiles, axis=1)
        x, v = star[0:3], star[3:6]
        swapped = jnp.concatenate([-v, -x, jnp.zeros((2, width), F32)], axis=0)
        terms = [term.astype(F32) for term in three_terms(swapped)]
        product = [term.astype(F32) for term in three_terms(x[0:1] * v[0:1] + x[1:2] * v[1:2] + x[2:3] * v[2:3])]
        last = jnp.concatenate([jnp.ones((3, width), F32)] + product + [jnp.zeros((2, width), F32)], axis=0)
        cross = jnp.concatenate(
            [terms[b] for unused, b in PAIRS] + [last, jnp.zeros((LANES - 56, width), F32)], axis=0
        ).astype(BF16)
        weighted = jnp.zeros((32, width), F32)
        radial = jnp.zeros((32, width), F32)
        for low in range(0, count, deep):
            here = slice(low, low + deep)
            rel = [jnp.concatenate([spread_ref[d, here, :]] * wide, axis=1) - x[d:d + 1] for d in range(3)]
            dist = rel[0] * rel[0] + rel[1] * rel[1] + (rel[2] * rel[2] + softening)
            inv = lax.rsqrt(dist)
            inv2 = inv * inv
            weight = inv * inv2
            dot = jnp.dot(factor_ref[here, :], cross, preferred_element_type=F32)
            turn = weight * inv2 * dot
            moment = moment_ref[:, here]
            weight_high, turn_high = weight.astype(BF16), turn.astype(BF16)
            weight_low = (weight - weight_high.astype(F32)).astype(BF16)
            turn_low = (turn - turn_high.astype(F32)).astype(BF16)
            weighted = weighted + jnp.dot(moment, weight_high, preferred_element_type=F32)
            weighted = weighted + jnp.dot(moment, weight_low, preferred_element_type=F32)
            radial = radial + jnp.dot(moment, turn_high, preferred_element_type=F32)
            radial = radial + jnp.dot(moment, turn_low, preferred_element_type=F32)
        weighted = weighted[0:8] + weighted[8:16] + weighted[16:24]
        radial = radial[0:8] + radial[8:16] + radial[16:24]
        acc = weighted[0:3] - x * weighted[6:7]
        jrk = weighted[3:6] - v * weighted[6:7] - 3.0 * (radial[0:3] - x * radial[6:7])
        for b in range(wide):
            for d in range(3):
                send_ref[0, pl.ds(d * blocks + block + b, 1), :] = acc[d:d + 1, b * LANES:(b + 1) * LANES]
                send_ref[0, pl.ds((3 + d) * blocks + block + b, 1), :] = jrk[d:d + 1, b * LANES:(b + 1) * LANES]

    def pair_of_parts(index, unused):
        part(index * (2 * wide))
        part(index * (2 * wide) + wide)
        for owner in range(owners // rounds):
            place(first_ref, states_ref, later, 1, index * (owners // rounds) + owner)
        return unused

    rounds = blocks // (2 * wide)
    lax.fori_loop(0, rounds, pair_of_parts, 0)
    for field in range(8):
        state_ref[field] = later[0:blocks, field, :]
    for peer in range(1, send_ref.shape[0]):
        send_ref[peer] = send_ref[0]


def forces(first, states, factor, moment, spread, blocks, peers):
    return pl.pallas_call(
        force_kernel,
        out_shape=(
            jax.ShapeDtypeStruct((peers, 6 * blocks, LANES), F32),
            jax.ShapeDtypeStruct((8, blocks, LANES), F32),
        ),
        in_specs=[hbm(), vmem(), hbm(), hbm(), hbm()],
        out_specs=(vmem(), vmem()),
        scratch_shapes=[
            pltpu.VMEM((blocks + 2, 8, LANES), F32),
            pltpu.VMEM((blocks + 2, 8, LANES), F32),
            pltpu.SMEM(first.shape, first.dtype),
            pltpu.VMEM(factor.shape, factor.dtype),
            pltpu.VMEM(moment.shape, moment.dtype),
            pltpu.VMEM(spread.shape, spread.dtype),
            pltpu.SemaphoreType.DMA((4,)),
        ],
        compiler_params=params(12),
        cost_estimate=cost(9),
        name="forces",
    )(pinned(first), states, pinned(factor), pinned(moment), pinned(spread))


def add_kernel(parts_ref, send_ref):
    total = jnp.sum(parts_ref[...], axis=0)
    send_ref[...] = jnp.broadcast_to(total[None], send_ref.shape)


def add_parts(parts, peers):
    return pl.pallas_call(
        add_kernel,
        out_shape=jax.ShapeDtypeStruct((peers,) + parts.shape[1:], F32),
        in_specs=[vmem()],
        out_specs=vmem(),
        compiler_params=params(4),
        name="add_parts",
    )(parts)


def correct_kernel(me_ref, first_ref, parts_ref, state_ref, own_ref, wide_ref):
    blocks = state_ref.shape[1]
    total = jnp.sum(parts_ref[...], axis=0)
    tau = state_ref[6]
    t2 = tau * tau
    for d in range(3):
        acc = total[d * blocks:(d + 1) * blocks]
        jrk = total[(3 + d) * blocks:(4 + d) * blocks]
        wide_ref[d, 0:blocks] = state_ref[d] + t2 * (0.15 * acc - tau * (jrk / 30.0))
        wide_ref[3 + d, 0:blocks] = state_ref[3 + d] + tau * (0.5 * acc - tau * (jrk / 12.0))
        wide_ref[6 + d, 0:blocks] = acc
        wide_ref[9 + d, 0:blocks] = jrk
    for f in range(12, 16):
        wide_ref[f, 0:blocks] = jnp.ones_like(tau)
    wide_ref[:, blocks:] = jnp.zeros((16, wide_ref.shape[1] - blocks, LANES), F32)
    start = first_ref[0, me_ref[0]]
    block = lax.shift_right_logical(start, 7)
    shift = lax.bitwise_and(start, LANES - 1)
    back = lax.bitwise_and(LANES - shift, LANES - 1)
    lane = iota((16, LANES), 1)
    low = pltpu.roll(wide_ref[:, block, :], back, 1)
    high = pltpu.roll(wide_ref[:, block + 1, :], back, 1)
    own_ref[...] = jnp.where(lane < LANES - shift, low, high)


def correct(me, first, parts, state):
    blocks = state.shape[1]
    return pl.pallas_call(
        correct_kernel,
        out_shape=(
            jax.ShapeDtypeStruct((16, LANES), F32),
            jax.ShapeDtypeStruct((16, blocks + 2, LANES), F32),
        ),
        in_specs=[smem(), smem(), vmem(), vmem()],
        out_specs=(vmem(), vmem()),
        compiler_params=params(4),
        name="correct",
    )(me, first, parts, state)


def permute_kernel(wide_ref, perm_ref, update_ref):
    blocks = perm_ref.shape[0] // LANES
    value = jnp.concatenate([wide_ref[:, block, :] for block in range(blocks)], axis=1)
    terms = jnp.concatenate(three_terms(value), axis=0)
    result = jnp.dot(terms, perm_ref[...], preferred_element_type=F32)
    update_ref[...] = (result[0:16] + result[16:32] + result[32:48])[0:12]


def permute(wide, perm):
    return pl.pallas_call(
        permute_kernel,
        out_shape=jax.ShapeDtypeStruct((12, perm.shape[1]), F32),
        in_specs=[vmem(), vmem()],
        out_specs=vmem(),
        compiler_params=params(8),
        cost_estimate=cost(2),
        name="permute",
    )(wide, perm)


def write_kernel(mine_ref, other_ref, here_ref, there_ref, pos_ref, vel_ref, acc_ref, jrk_ref,
                 new_pos_ref, new_vel_ref, new_acc_ref, new_jrk_ref):
    count = pos_ref.shape[1]
    both = jnp.concatenate([mine_ref[:, 0:SLOTS], other_ref[:, 0:SLOTS]], axis=1)
    place = jnp.concatenate([here_ref[...], there_ref[...]], axis=0)[:, 0:1]
    onehot = jnp.where(iota((2 * SLOTS, count), 1) == place, 1.0, 0.0).astype(BF16)
    values = jnp.dot(jnp.concatenate(three_terms(both), axis=0), onehot, preferred_element_type=F32)
    values = values[0:16] + values[16:32] + values[32:48]
    hit = values[12:13] > 0.5
    new_pos_ref[...] = jnp.where(hit, values[0:3], pos_ref[...])
    new_vel_ref[...] = jnp.where(hit, values[3:6], vel_ref[...])
    new_acc_ref[...] = jnp.where(hit, values[6:9], acc_ref[...])
    new_jrk_ref[...] = jnp.where(hit, values[9:12], jrk_ref[...])


def write(mine, other, here, there, position, velocity, accel, jerk_old):
    shape = jax.ShapeDtypeStruct(position.shape, F32)
    return pl.pallas_call(
        write_kernel,
        out_shape=(shape,) * 4,
        in_specs=[vmem()] * 8,
        out_specs=(vmem(),) * 4,
        compiler_params=params(4),
        name="write",
    )(mine, other, here, there, position, velocity, accel, jerk_old)


def swap(value):
    return lax.ppermute(value, "core", [(0, 1), (1, 0)])


def exchange(value, axes):
    return lax.all_to_all(value, axes, 0, 0, tiled=True)


def local(owners, plane, depth, position, velocity, accel, jerk_old, masses, phase, levels, active):
    count = position.shape[1]
    blocks = active.shape[0]
    me = lax.axis_index(SRC).reshape(1).astype(jnp.int32)
    send, source, mine = pick(
        me, position, velocity, accel, jerk_old, masses.reshape(1, count), phase.reshape(1, count),
        levels.reshape(1, count), active, owners,
    )
    states = exchange(send, SRC)
    other = swap(mine)
    first, factor, moment, spread = prepare(source, active)
    perm = tables(active, count)
    states, other, perm = lax.optimization_barrier((states, other, perm))
    send, state = forces(first, states, factor, moment, spread, blocks, plane)
    parts = exchange(add_parts(exchange(send, PLANE), depth), "z")
    own, wide = correct(me, first, parts, state)
    update = permute(wide, perm)
    new = write(own, swap(own), mine, other, position, velocity, accel, jerk_old)
    return new + (update,)


def solution(mesh):
    owners = mesh.shape["src"]
    plane = 16
    depth = owners // plane
    fine = Mesh(mesh.devices.reshape(depth, 4, 4, mesh.shape["act"]), ("z", "y", "x", "core"))
    stars = P(None, SRC)
    placed = (stars,) * 4 + (P(SRC),) * 3 + (P("core", None),)
    return jax.shard_map(
        lambda *arrays: local(owners, plane, depth, *arrays),
        mesh=fine,
        in_specs=placed,
        out_specs=(stars,) * 4 + (P(None, "core"),),
        check_vma=False,
    )
```

time: 100 us -> 77.1 us (0.77)
  Pallas kernels: 39.3 us -> 19.5 us
  blocking collectives: 25.3 us -> 23.4 us
  waiting for transfers between devices: 9.4 us -> 10.7 us
  local copies, waits for them, and re-layouts: 2 us -> 0.72 us
  starting transfers between devices: 22.8 us -> 21.6 us
    pallas_call x1, Pallas kernels: 21.4 us -> 8.68 us  [forces(): pl.pallas_call(force_kernel, out_shape=(jax.ShapeDtypeStruct((peers, 6 *...]
    pallas_call x2 -> x4, Pallas kernels: 11.6 us -> 7.6 us  [the longest x1 4.08 us: prepare(): pl.pallas_call(prepare_kernel, out_shape=(jax.ShapeDtypeStruct((1, LANES)...]
    all_to_all x1, waiting for transfers between devices: 7.29 us -> 10.7 us  [exchange(): return lax.all_to_all(value, axes, 0, 0, tiled=True)]
    ppermute x2, waiting for transfers between devices: 2.11 us -> 0.01 us  [swap(): return lax.ppermute(value, 'core', [(0, 1), (1, 0)])]
    all_to_all x2, blocking collectives: 25.3 us -> 23.4 us  [exchange(): return lax.all_to_all(value, axes, 0, 0, tiled=True)]
    pallas_call x1, Pallas kernels: 1.69 us -> 0.03 us  [add_parts(): pl.pallas_call(add_kernel, out_shape=jax.ShapeDtypeStruct((peers,) + part...]
    unnamed x6 -> x14, local copies, waits for them, and re-layouts: 2 us -> 0.72 us
    pallas_call x1, Pallas kernels: 2.15 us -> 0.94 us  [write(): pl.pallas_call(write_kernel, out_shape=(shape,) * 4, in_specs=[vmem()] *...]
  transfers between devices with their start and end apart: 3 -> 3, of which waited for: 3 -> 1; matrix products, arithmetic and copies ran while one was open for 0% -> 0% of each run, Pallas kernels for 8% -> 9%
where the time goes in v2:
time: 77.1 us; the launch traced here: 76.7 us
  blocking collectives  23.4 us (30%)
  starting transfers between devices  21.6 us (28%)
  Pallas kernels  19.5 us (25%)
  waiting for transfers between devices  10.7 us (14%)
    all_to_all x2, blocking collectives, exchange(): return lax.all_to_all(value, axes, 0, 0, tiled=True)  23.4 us
    all_to_all x1, starting transfers between devices, exchange(): return lax.all_to_all(value, axes, 0, 0, tiled=True)  16.3 us
    all_to_all x1, waiting for transfers between devices, exchange(): return lax.all_to_all(value, axes, 0, 0, tiled=True)  10.7 us
    pallas_call x1, Pallas kernels, forces(): pl.pallas_call(force_kernel, out_shape=(jax.ShapeDtypeStruct((peers, 6 *...  8.68 us
    ppermute x2, starting transfers between devices, swap(): return lax.ppermute(value, 'core', [(0, 1), (1, 0)])  5.31 us
    pallas_call x1, Pallas kernels, prepare(): pl.pallas_call(prepare_kernel, out_shape=(jax.ShapeDtypeStruct((1, LANES)...  4.08 us
    pallas_call x1, Pallas kernels, pick(): pl.pallas_call(pick_kernel, out_shape=(jax.ShapeDtypeStruct((owners, 8, L...  2.24 us
    pallas_call x1, Pallas kernels, tables(): pl.pallas_call(lambda *refs: tables_kernel(count, *refs), out_shape=jax.S...  1.78 us
  transfers between devices with their start and end apart: 3, of which 1 were waited for; matrix products, arithmetic and copies ran while one was open for 0% of the time, Pallas kernels for 9%

profile of v2, /device:TPU:1, one launch (start us, length us, event | category | flops | bytes accessed | tf_op | source)
XLA Modules:
  0.0 76.7 jit_solution(10776658177155703225)
XLA Ops:
  0.6 2.2 %pick.1 = (f32[128,8,128]{2,1,0:T(8,128)}, f32[8,2048]{1,0:T(8,128)}, s32[64,128]{1,0:T(8,128)}) custom-call(s32[1]{0:T(128)} %bitcast.me_ref, f32[3,2048]{1,0:T(4,128)} %pos_ref.3, f32[3,2048]{1,0:T(4,128)} %vel_ref.3, f32[3,2048]{1,0:T(4,128)} %acc_ref.3, f32[3,2048]{1,0:T(4,128)} %jrk_ref.3, f32[1,2048]{1,0:T(1,128)} %bitcast.4, f32[1,2048]{1,0:T(1,128)} %bitcast.5, ...), custom_call_target="tpu_custom_call" | custom-call | tf_op jit(solution)/shard_map/pick/pallas_call | solution.py:97
  2.9 16.3 %all-to-all-start = ((f32[128,8,128]{2,1,0:T(8,128)}), f32[128,8,128]{2,1,0:T(8,128)S(1)}, u32[]{:S(2)}, u32[]{:S(2)}) async-start(f32[128,8,128]{2,1,0:T(8,128)} %get-tuple-element.25), calls=%async_computation | async-start | bytes 1048576 | tf_op jit(solution)/shard_map/all_to_all | solution.py:414
  19.2 1.0 %collective-permute-start = (s32[64,128]{1,0:T(8,128)}, s32[64,128]{1,0:T(8,128)S(1)}, u32[]{:S(2)}, u32[]{:S(2)}) collective-permute-start(s32[64,128]{1,0:T(8,128)} %get-tuple-element.26.here_ref), channel_id=1, source_target_pairs={{0,1},{1,0},{2,3},{3,2},{4,5},{5,4},{6,7},{7,6},{8,9},{9,8},{10,11... | collective-permute-start | bytes 98312 | tf_op jit(solution)/shard_map/ppermute | solution.py:410
  20.3 0.0 copy-start.4
  20.3 0.7 copy-done.4
  21.0 1.8 %tables.1.perm_ref = bf16[1024,1024]{1,0:T(8,128)(2,1)S(1)} custom-call(s32[8,128]{1,0:T(8,128)S(1)} %copy-done.4), custom_call_target="tpu_custom_call" | custom-call | bytes 12000000 | tf_op jit(solution)/shard_map/tables/pallas_call | solution.py:196
  22.8 4.1 %prepare.1 = (s32[1,128]{1,0:T(1,128)}, bf16[2048,128]{1,0:T(8,128)(2,1)}, bf16[32,2048]{1,0:T(8,128)(2,1)}, f32[3,2048,128]{2,1,0:T(8,128)}) custom-call(f32[8,2048]{1,0:T(8,128)} %get-tuple-element.23.source_ref, s32[8,128]{1,0:T(8,128)} %refs_0_.1), custom_call_target="tpu_custom_call" | custom-call | bytes 15000000 | tf_op jit(solution)/shard_map/prepare/pallas_call | solution.py:152
  26.8 0.0 copy-start.6
  26.8 0.0 collective-permute-done.there_ref
  26.8 10.7 %all-to-all-done.states_ref = f32[128,8,128]{2,1,0:T(8,128)S(1)} async-done(((f32[128,8,128]{2,1,0:T(8,128)}), f32[128,8,128]{2,1,0:T(8,128)S(1)}, u32[]{:S(2)}, u32[]{:S(2)}) %all-to-all-start) | async-done | bytes 524320 | tf_op jit(solution)/shard_map/all_to_all | solution.py:414
  37.5 8.7 %forces.1 = (f32[16,48,128]{2,1,0:T(8,128)S(1)}, f32[8,8,128]{2,1,0:T(8,128)S(1)}) custom-call(s32[1,128]{1,0:T(1,128)} %get-tuple-element.24.first_hbm.first_ref, f32[128,8,128]{2,1,0:T(8,128)S(1)} %all-to-all-done.states_ref, bf16[2048,128]{1,0:T(8,128)(2,1)} %get-tuple-element.28.factor_hbm, bf16[32,2048]{1,0:T(8,128)(2,1)} %get-tuple-element.29.moment_hbm, ...), custom_call_target="tpu_custom_call" | custom-call | bytes 27000000 | tf_op jit(solution)/shard_map/forces/pallas_call | solution.py:283
  46.2 0.0 copy-start
  46.2 0.0 copy-start.1
  46.2 0.0 copy-start.2
  46.2 0.0 copy-start.3
  46.3 0.0 copy-start.5
  46.3 11.3 %all_to_all.15.parts_ref = f32[16,48,128]{2,1,0:T(8,128)S(1)} all-to-all(f32[16,48,128]{2,1,0:T(8,128)S(1)} %get-tuple-element.31), channel_id=1, replica_groups=mesh['z'=8,'y'=4,'x'=4,'core'=2] {'y','x'}, dimensions={0} | all-to-all | bytes 786432 | tf_op jit(solution)/shard_map/all_to_all | solution.py:414
  57.5 12.1 %all_to_all.16.parts_ref = f32[8,48,128]{2,1,0:T(8,128)S(1)} all-to-all(f32[8,48,128]{2,1,0:T(8,128)S(1)} %add_parts.1), channel_id=1, replica_groups=mesh['z'=8,'y'=4,'x'=4,'core'=2] {'z'}, dimensions={0} | all-to-all | bytes 393216 | tf_op jit(solution)/shard_map/all_to_all | solution.py:414
  69.7 0.0 copy-done.6
  69.7 0.6 correct.1
  70.3 4.3 %collective-permute-start.1 = (f32[16,128]{1,0:T(8,128)S(1)}, f32[16,128]{1,0:T(8,128)S(1)}, u32[]{:S(2)}, u32[]{:S(2)}) collective-permute-start(f32[16,128]{1,0:T(8,128)S(1)} %get-tuple-element.33.mine_ref), channel_id=1, source_target_pairs={{0,1},{1,0},{2,3},{3,2},{4,5},{5,4},{6,7},{7,6},{8,9},{9,8},{10,11... | collective-permute-start | bytes 24584 | tf_op jit(solution)/shard_map/ppermute | solution.py:410
  74.6 1.1 %permute.1 = f32[12,1024]{1,0:T(8,128)} custom-call(f32[16,10,128]{2,1,0:T(8,128)S(1)} %get-tuple-element.39.wide_ref, bf16[1024,1024]{1,0:T(8,128)(2,1)S(1)} %tables.1.perm_ref), custom_call_target="tpu_custom_call" | custom-call | bytes 6000000 | tf_op jit(solution)/shard_map/permute/pallas_call | solution.py:371
  75.7 0.0 collective-permute-done.1.other_ref
  75.7 0.0 copy-done
  75.7 0.0 copy-done.1
  75.7 0.0 copy-done.2
  75.7 0.0 copy-done.3
  75.7 0.0 copy-done.5
  75.7 0.9 %write.1 = (f32[3,2048]{1,0:T(4,128)}, f32[3,2048]{1,0:T(4,128)}, f32[3,2048]{1,0:T(4,128)}, f32[3,2048]{1,0:T(4,128)}) custom-call(f32[16,128]{1,0:T(8,128)S(1)} %get-tuple-element.33.mine_ref, f32[16,128]{1,0:T(8,128)S(1)} %collective-permute-done.1.other_ref, s32[64,128]{1,0:T(8,128)S(1)} %copy-done.5, s32[64,128]{1,0:T(8,128)S(1)} %collective-permute-done.there_ref, ...), custom_call_target="tpu_custom_call" | custom-call | tf_op jit(solution)/shard_map/write/pallas_call | solution.py:399
  (1 shorter events, 0.0 us)
Async XLA Ops:
  2.9 34.6 %all-to-all-start = ((f32[128,8,128]{2,1,0:T(8,128)}), f32[128,8,128]{2,1,0:T(8,128)S(1)}, u32[]{:S(2)}, u32[]{:S(2)}) async-start(f32[128,8,128]{2,1,0:T(8,128)} %get-tuple-element.25), calls=%async_computation | async-start | bytes 1048576 | tf_op jit(solution)/shard_map/all_to_all | solution.py:414
  19.2 7.6 %collective-permute-start = (s32[64,128]{1,0:T(8,128)}, s32[64,128]{1,0:T(8,128)S(1)}, u32[]{:S(2)}, u32[]{:S(2)}) collective-permute-start(s32[64,128]{1,0:T(8,128)} %get-tuple-element.26.here_ref), channel_id=1, source_target_pairs={{0,1},{1,0},{2,3},{3,2},{4,5},{5,4},{6,7},{7,6},{8,9},{9,8},{10,11... | collective-permute-start | bytes 98312 | tf_op jit(solution)/shard_map/ppermute | solution.py:410
  20.3 0.7 copy-start.4
  26.8 42.9 %copy-start.6 = (s32[1,128]{1,0:T(1,128)S(1)}, s32[1,128]{1,0:T(1,128)}, u32[]{:S(2)}) copy-start(s32[1,128]{1,0:T(1,128)} %get-tuple-element.24.first_hbm.first_ref) | copy-start | bytes 1540
  46.2 29.5 %copy-start = (f32[3,2048]{1,0:T(4,128)S(1)}, f32[3,2048]{1,0:T(4,128)}, u32[]{:S(2)}) copy-start(f32[3,2048]{1,0:T(4,128)} %pos_ref.3) | copy-start | bytes 73732
  46.2 29.5 %copy-start.1 = (f32[3,2048]{1,0:T(4,128)S(1)}, f32[3,2048]{1,0:T(4,128)}, u32[]{:S(2)}) copy-start(f32[3,2048]{1,0:T(4,128)} %vel_ref.3) | copy-start | bytes 73732
  46.2 29.5 %copy-start.2 = (f32[3,2048]{1,0:T(4,128)S(1)}, f32[3,2048]{1,0:T(4,128)}, u32[]{:S(2)}) copy-start(f32[3,2048]{1,0:T(4,128)} %acc_ref.3) | copy-start | bytes 73732
  46.2 29.5 %copy-start.3 = (f32[3,2048]{1,0:T(4,128)S(1)}, f32[3,2048]{1,0:T(4,128)}, u32[]{:S(2)}) copy-start(f32[3,2048]{1,0:T(4,128)} %jrk_ref.3) | copy-start | bytes 73732
  46.3 29.5 %copy-start.5 = (s32[64,128]{1,0:T(8,128)S(1)}, s32[64,128]{1,0:T(8,128)}, u32[]{:S(2)}) copy-start(s32[64,128]{1,0:T(8,128)} %get-tuple-element.26.here_ref) | copy-start | bytes 98308
  70.3 5.4 %collective-permute-start.1 = (f32[16,128]{1,0:T(8,128)S(1)}, f32[16,128]{1,0:T(8,128)S(1)}, u32[]{:S(2)}, u32[]{:S(2)}) collective-permute-start(f32[16,128]{1,0:T(8,128)S(1)} %get-tuple-element.33.mine_ref), channel_id=1, source_target_pairs={{0,1},{1,0},{2,3},{3,2},{4,5},{5,4},{6,7},{7,6},{8,9},{9,8},{10,11... | collective-permute-start | bytes 24584 | tf_op jit(solution)/shard_map/ppermute | solution.py:410

commit v3 on v2

--- a/solution.py
+++ b/solution.py
@@ -8,12 +8,13 @@
 
 softening = 0.0025
 SLOTS = 64
+ROWS = 7
 LANES = 128
 PLANE = ("y", "x")
 SRC = ("z", "y", "x")
 F32 = jnp.float32
 BF16 = jnp.bfloat16
-PREP = 56
+PREP = 12
 PAIRS = ((0, 0), (0, 1), (1, 0), (1, 1), (0, 2), (2, 0))
 
 
@@ -88,8 +89,10 @@
     terms = jnp.concatenate(three_terms(table), axis=0)
     picked = lax.dot_general(terms, onehot, (((1,), (1,)), ((), ())), preferred_element_type=F32)
     picked = picked[0:16] + picked[16:32] + picked[32:48]
-    block = jnp.concatenate([picked[0:8], picked[8:16]], axis=1)
-    send_ref[...] = jnp.broadcast_to(block[None], send_ref.shape)
+    block = jnp.concatenate([picked[0:8], picked[8:16]], axis=1)[0:ROWS]
+    blocks = jnp.concatenate([block] * 8, axis=0)
+    for piece in range(send_ref.shape[0] // (8 * ROWS)):
+        send_ref[piece * 8 * ROWS:(piece + 1) * 8 * ROWS] = blocks
 
 
 def pick(me, position, velocity, accel, jerk_old, masses, phase, levels, active, owners):
@@ -97,7 +100,7 @@
     return pl.pallas_call(
         pick_kernel,
         out_shape=(
-            jax.ShapeDtypeStruct((owners, 8, LANES), F32),
+            jax.ShapeDtypeStruct((owners * ROWS, LANES), F32),
             jax.ShapeDtypeStruct((8, count), F32),
             jax.ShapeDtypeStruct((SLOTS, LANES), jnp.int32),
         ),
@@ -114,7 +117,7 @@
     return (owner * (rows * LANES) + iota((rows, LANES), 0) * LANES + iota((rows, LANES), 1)).astype(F32)
 
 
-def prepare_kernel(source_ref, active_ref, first_ref, factor_ref, moment_ref, spread_ref):
+def prepare_kernel(source_ref, active_ref, first_ref, factor_ref, moment_ref):
     count = source_ref.shape[1]
     rows = active_ref.shape[0]
     total = rows * LANES
@@ -142,9 +145,6 @@
         here = slice(piece * LANES, (piece + 1) * LANES)
         across = jnp.transpose(stack[:, here])
         factor_ref[here, :] = jnp.concatenate([across, jnp.zeros((LANES, LANES - 56), F32)], axis=1).astype(BF16)
-        across = jnp.transpose(source[:, here])
-        for field in range(3):
-            spread_ref[field, here, :] = jnp.broadcast_to(across[:, field:field + 1], (LANES, LANES))
 
 
 def prepare(source, active):
@@ -155,10 +155,9 @@
             jax.ShapeDtypeStruct((1, LANES), jnp.int32),
             jax.ShapeDtypeStruct((count, LANES), BF16),
             jax.ShapeDtypeStruct((32, count), BF16),
-            jax.ShapeDtypeStruct((3, count, LANES), F32),
         ),
         in_specs=[vmem()] * 2,
-        out_specs=(vmem(),) * 4,
+        out_specs=(vmem(),) * 3,
         compiler_params=params(PREP),
         cost_estimate=cost(5),
         name="prepare",
@@ -169,7 +168,12 @@
     start = first_ref[0, owner]
     block = lax.shift_right_logical(start, 7)
     shift = lax.bitwise_and(start, LANES - 1)
-    turned = pltpu.roll(states_ref[owner], lax.bitwise_and(shift + half * SLOTS, LANES - 1), 1)
+    low = owner * ROWS
+    if low + 8 <= states_ref.shape[0]:
+        value = states_ref[low:low + 8]
+    else:
+        value = jnp.concatenate([states_ref[low:low + ROWS], jnp.zeros((8 - ROWS, LANES), F32)], axis=0)
+    turned = pltpu.roll(value, lax.bitwise_and(shift + half * SLOTS, LANES - 1), 1)
     pltpu.store(compact.at[block], turned, mask=iota((8, LANES), 1) >= shift)
     compact[block + 1] = turned
 
@@ -204,24 +208,31 @@
     )(active)
 
 
-def force_kernel(first_hbm, states_ref, factor_hbm, moment_hbm, spread_hbm, send_ref, state_ref,
-                 compact, later, first_ref, factor_ref, moment_ref, spread_ref, arrived):
-    owners = states_ref.shape[0]
-    count = spread_ref.shape[1]
+def force_kernel(first_hbm, states_ref, factor_ref, moment_ref, send_ref, state_ref,
+                 compact, later, first_ref, spread_ref, arrived):
+    owners = states_ref.shape[0] // ROWS
+    count = factor_ref.shape[0]
     blocks = send_ref.shape[1] // 6
-    pairs = ((first_hbm, first_ref), (factor_hbm, factor_ref), (moment_hbm, moment_ref), (spread_hbm, spread_ref))
-    copies = [pltpu.make_async_copy(here, there, arrived.at[i]) for i, (here, there) in enumerate(pairs)]
-    for copy in copies:
-        copy.start()
-    copies[0].wait()
-
-    def place_early(owner, unused):
+    copy = pltpu.make_async_copy(first_hbm, first_ref, arrived)
+    copy.start()
+    row, column = iota((LANES, 3 * LANES), 0), iota((LANES, 3 * LANES), 1)
+    coordinate = lax.shift_right_logical(column, 7)
+    gather = (row == coordinate) | (row == coordinate + 16) | (row == coordinate + 40)
+    gather = jnp.where(gather, 1.0, 0.0).astype(BF16)
+
+    def spread(low, size):
+        here = pl.ds(low, size)
+        wide = jnp.dot(factor_ref[here, :], gather, preferred_element_type=F32)
+        for d in range(3):
+            spread_ref[d, here, :] = wide[:, d * LANES:(d + 1) * LANES]
+
+    size = count // 8
+    spread(0, 4 * size)
+    copy.wait()
+
+    spread(4 * size, 4 * size)
+    for owner in range(owners):
         place(first_ref, states_ref, compact, 0, owner)
-        return unused
-
-    lax.fori_loop(0, owners, place_early, 0, unroll=16)
-    for copy in copies[1:]:
-        copy.wait()
     wide, deep = 2, min(1024, count)
     width = wide * LANES
 
@@ -264,43 +275,37 @@
                 send_ref[0, pl.ds(d * blocks + block + b, 1), :] = acc[d:d + 1, b * LANES:(b + 1) * LANES]
                 send_ref[0, pl.ds((3 + d) * blocks + block + b, 1), :] = jrk[d:d + 1, b * LANES:(b + 1) * LANES]
 
-    def pair_of_parts(index, unused):
-        part(index * (2 * wide))
-        part(index * (2 * wide) + wide)
-        for owner in range(owners // rounds):
-            place(first_ref, states_ref, later, 1, index * (owners // rounds) + owner)
-        return unused
-
-    rounds = blocks // (2 * wide)
-    lax.fori_loop(0, rounds, pair_of_parts, 0)
+    for step, block in enumerate(range(0, blocks, wide)):
+        part(block)
+        share = owners * wide // blocks
+        for owner in range(step * share, (step + 1) * share):
+            place(first_ref, states_ref, later, 1, owner)
     for field in range(8):
         state_ref[field] = later[0:blocks, field, :]
     for peer in range(1, send_ref.shape[0]):
         send_ref[peer] = send_ref[0]
 
 
-def forces(first, states, factor, moment, spread, blocks, peers):
+def forces(first, states, factor, moment, blocks, peers):
     return pl.pallas_call(
         force_kernel,
         out_shape=(
             jax.ShapeDtypeStruct((peers, 6 * blocks, LANES), F32),
             jax.ShapeDtypeStruct((8, blocks, LANES), F32),
         ),
-        in_specs=[hbm(), vmem(), hbm(), hbm(), hbm()],
+        in_specs=[hbm(), vmem(), vmem(), vmem()],
         out_specs=(vmem(), vmem()),
         scratch_shapes=[
             pltpu.VMEM((blocks + 2, 8, LANES), F32),
             pltpu.VMEM((blocks + 2, 8, LANES), F32),
             pltpu.SMEM(first.shape, first.dtype),
-            pltpu.VMEM(factor.shape, factor.dtype),
-            pltpu.VMEM(moment.shape, moment.dtype),
-            pltpu.VMEM(spread.shape, spread.dtype),
-            pltpu.SemaphoreType.DMA((4,)),
+            pltpu.VMEM((3, factor.shape[0], LANES), F32),
+            pltpu.SemaphoreType.DMA,
         ],
         compiler_params=params(12),
         cost_estimate=cost(9),
         name="forces",
-    )(pinned(first), states, pinned(factor), pinned(moment), pinned(spread))
+    )(pinned(first), states, factor, moment)
 
 
 def add_kernel(parts_ref, send_ref):
@@ -422,12 +427,12 @@
         me, position, velocity, accel, jerk_old, masses.reshape(1, count), phase.reshape(1, count),
         levels.reshape(1, count), active, owners,
     )
-    states = exchange(send, SRC)
+    states = exchange(send.reshape(owners, ROWS, 1, LANES), SRC).reshape(send.shape)
     other = swap(mine)
-    first, factor, moment, spread = prepare(source, active)
+    first, factor, moment = prepare(source, active)
     perm = tables(active, count)
     states, other, perm = lax.optimization_barrier((states, other, perm))
-    send, state = forces(first, states, factor, moment, spread, blocks, plane)
+    send, state = forces(first, states, factor, moment, blocks, plane)
     parts = exchange(add_parts(exchange(send, PLANE), depth), "z")
     own, wide = correct(me, first, parts, state)
     update = permute(wide, perm)

time: 77.1 us -> 74.9 us (0.971)
  Pallas kernels: 19.5 us -> 14.9 us
  waiting for transfers between devices: 10.7 us -> 12.3 us
    pallas_call x1, Pallas kernels: 4.08 us -> 0.49 us  [prepare(): pl.pallas_call(prepare_kernel, out_shape=(jax.ShapeDtypeStruct((1, LANES)...]
    all_to_all x1, waiting for transfers between devices: 10.7 us -> 12.3 us  [exchange(): return lax.all_to_all(value, axes, 0, 0, tiled=True)]
    pallas_call x1, Pallas kernels: 8.68 us -> 7.71 us  [forces(): pl.pallas_call(force_kernel, out_shape=(jax.ShapeDtypeStruct((peers, 6 *...]
  transfers between devices with their start and end apart: 3 -> 3, of which waited for: 1 -> 1; matrix products, arithmetic and copies ran while one was open for 0% -> 0% of each run, Pallas kernels for 9% -> 5%
where the time goes in v3:
time: 74.9 us; the launch traced here: 74.4 us
  blocking collectives  23.3 us (31%)
  starting transfers between devices  21.9 us (29%)
  Pallas kernels  14.9 us (20%)
  waiting for transfers between devices  12.3 us (16%)
  local copies, waits for them, and re-layouts  1.24 us (2%)
  between operations  0.78 us (1%)
    all_to_all x2, blocking collectives, exchange(): return lax.all_to_all(value, axes, 0, 0, tiled=True)  23.3 us
    all_to_all x1, starting transfers between devices, exchange(): return lax.all_to_all(value, axes, 0, 0, tiled=True)  16.5 us
    all_to_all x1, waiting for transfers between devices, exchange(): return lax.all_to_all(value, axes, 0, 0, tiled=True)  12.3 us
    pallas_call x1, Pallas kernels, forces(): pl.pallas_call(force_kernel, out_shape=(jax.ShapeDtypeStruct((peers, 6 *...  7.71 us
    ppermute x2, starting transfers between devices, swap(): return lax.ppermute(value, 'core', [(0, 1), (1, 0)])  5.42 us
    pallas_call x1, Pallas kernels, pick(): pl.pallas_call(pick_kernel, out_shape=(jax.ShapeDtypeStruct((owners * ROW...  2.21 us
    pallas_call x1, Pallas kernels, tables(): pl.pallas_call(lambda *refs: tables_kernel(count, *refs), out_shape=jax.S...  1.78 us
  transfers between devices with their start and end apart: 3, of which 1 were waited for; matrix products, arithmetic and copies ran while one was open for 0% of the time, Pallas kernels for 5%

profile of v3, /device:TPU:1, one launch (start us, length us, event | category | flops | bytes accessed | tf_op | source)
XLA Modules:
  0.0 74.4 jit_solution(8050673916351909197)
XLA Ops:
  0.6 0.0 copy-start.6
  0.7 2.2 %pick.1 = (f32[896,128]{1,0:T(8,128)}, f32[8,2048]{1,0:T(8,128)}, s32[64,128]{1,0:T(8,128)}) custom-call(s32[1]{0:T(128)} %bitcast.me_ref, f32[3,2048]{1,0:T(4,128)} %pos_ref.3, f32[3,2048]{1,0:T(4,128)} %vel_ref.3, f32[3,2048]{1,0:T(4,128)} %acc_ref.3, f32[3,2048]{1,0:T(4,128)} %jrk_ref.3, f32[1,2048]{1,0:T(1,128)} %bitcast.8, f32[1,2048]{1,0:T(1,128)} %bitcast.9, ...), custom_call_target="tpu_custom_call" | custom-call | tf_op jit(solution)/shard_map/pick/pallas_call | solution.py:100
  2.9 0.0 copy-start.4
  2.9 16.5 %all-to-all-start = ((f32[128,7,1,128]{3,2,1,0:T(1,128)}), f32[128,7,1,128]{3,2,1,0:T(1,128)S(1)}, u32[]{:S(2)}, u32[]{:S(2)}) async-start(f32[128,7,1,128]{3,2,1,0:T(1,128)} %bitcast.7), calls=%async_computation | async-start | bytes 917504 | tf_op jit(solution)/shard_map/all_to_all | solution.py:419
  19.3 1.2 %collective-permute-start = (s32[64,128]{1,0:T(8,128)}, s32[64,128]{1,0:T(8,128)S(1)}, u32[]{:S(2)}, u32[]{:S(2)}) collective-permute-start(s32[64,128]{1,0:T(8,128)} %get-tuple-element.25.here_ref), channel_id=1, source_target_pairs={{0,1},{1,0},{2,3},{3,2},{4,5},{5,4},{6,7},{7,6},{8,9},{9,8},{10,11... | collective-permute-start | bytes 98312 | tf_op jit(solution)/shard_map/ppermute | solution.py:415
  20.6 0.0 copy-start.5
  20.6 0.7 copy-done.5
  21.3 1.8 %tables.1.perm_ref = bf16[1024,1024]{1,0:T(8,128)(2,1)S(1)} custom-call(s32[8,128]{1,0:T(8,128)S(1)} %copy-done.5), custom_call_target="tpu_custom_call" | custom-call | bytes 12000000 | tf_op jit(solution)/shard_map/tables/pallas_call | solution.py:200
  23.0 0.0 copy-done.6
  23.1 0.0 copy-done.4
  23.1 0.5 prepare.1
  23.6 0.0 copy-start.8
  23.6 0.5 copy-done.8
  24.1 0.0 collective-permute-done.there_ref
  24.1 0.0 copy-start.9
  24.1 12.3 %all-to-all-done = f32[128,7,1,128]{3,2,1,0:T(1,128)S(1)} async-done(((f32[128,7,1,128]{3,2,1,0:T(1,128)}), f32[128,7,1,128]{3,2,1,0:T(1,128)S(1)}, u32[]{:S(2)}, u32[]{:S(2)}) %all-to-all-start) | async-done | bytes 458784 | tf_op jit(solution)/shard_map/all_to_all | solution.py:419
  36.4 7.7 %forces.1 = (f32[16,48,128]{2,1,0:T(8,128)S(1)}, f32[8,8,128]{2,1,0:T(8,128)S(1)}) custom-call(s32[1,128]{1,0:T(1,128)} %copy-done.8, f32[896,128]{1,0:T(8,128)S(1)} %bitcast.6, bf16[2048,128]{1,0:T(8,128)(2,1)S(1)} %get-tuple-element.27.factor_ref, bf16[32,2048]{1,0:T(8,128)(2,1)S(1)} %get-tuple-element.28.moment_ref), custom_call_target="tpu_custom_call" | custom-call | bytes 27000000 | tf_op jit(solution)/shard_map/forces/pallas_call | solution.py:290
  44.1 0.0 copy-start
  44.1 0.0 copy-start.1
  44.2 0.0 copy-start.2
  44.2 0.0 copy-start.3
  44.2 0.0 copy-start.7
  44.2 11.1 %all_to_all.15.parts_ref = f32[16,48,128]{2,1,0:T(8,128)S(1)} all-to-all(f32[16,48,128]{2,1,0:T(8,128)S(1)} %get-tuple-element.29), channel_id=1, replica_groups=mesh['z'=8,'y'=4,'x'=4,'core'=2] {'y','x'}, dimensions={0} | all-to-all | bytes 786432 | tf_op jit(solution)/shard_map/all_to_all | solution.py:419
  55.4 12.2 %all_to_all.16.parts_ref = f32[8,48,128]{2,1,0:T(8,128)S(1)} all-to-all(f32[8,48,128]{2,1,0:T(8,128)S(1)} %add_parts.1), channel_id=1, replica_groups=mesh['z'=8,'y'=4,'x'=4,'core'=2] {'z'}, dimensions={0} | all-to-all | bytes 393216 | tf_op jit(solution)/shard_map/all_to_all | solution.py:419
  67.5 0.0 copy-done.9
  67.5 0.6 correct.1
  68.2 4.2 %collective-permute-start.1 = (f32[16,128]{1,0:T(8,128)S(1)}, f32[16,128]{1,0:T(8,128)S(1)}, u32[]{:S(2)}, u32[]{:S(2)}) collective-permute-start(f32[16,128]{1,0:T(8,128)S(1)} %get-tuple-element.31.mine_ref), channel_id=1, source_target_pairs={{0,1},{1,0},{2,3},{3,2},{4,5},{5,4},{6,7},{7,6},{8,9},{9,8},{10,11... | collective-permute-start | bytes 24584 | tf_op jit(solution)/shard_map/ppermute | solution.py:415
  72.4 1.1 %permute.1 = f32[12,1024]{1,0:T(8,128)} custom-call(f32[16,10,128]{2,1,0:T(8,128)S(1)} %get-tuple-element.37.wide_ref, bf16[1024,1024]{1,0:T(8,128)(2,1)S(1)} %tables.1.perm_ref), custom_call_target="tpu_custom_call" | custom-call | bytes 6000000 | tf_op jit(solution)/shard_map/permute/pallas_call | solution.py:376
  73.5 0.0 collective-permute-done.1.other_ref
  73.5 0.0 copy-done
  73.5 0.0 copy-done.1
  73.5 0.0 copy-done.2
  73.5 0.0 copy-done.3
  73.5 0.0 copy-done.7
  73.5 0.9 %write.1 = (f32[3,2048]{1,0:T(4,128)}, f32[3,2048]{1,0:T(4,128)}, f32[3,2048]{1,0:T(4,128)}, f32[3,2048]{1,0:T(4,128)}) custom-call(f32[16,128]{1,0:T(8,128)S(1)} %get-tuple-element.31.mine_ref, f32[16,128]{1,0:T(8,128)S(1)} %collective-permute-done.1.other_ref, s32[64,128]{1,0:T(8,128)S(1)} %copy-done.7, s32[64,128]{1,0:T(8,128)S(1)} %collective-permute-done.there_ref, ...), custom_call_target="tpu_custom_call" | custom-call | tf_op jit(solution)/shard_map/write/pallas_call | solution.py:404
  (1 shorter events, 0.0 us)
Async XLA Ops:
  0.6 22.4 %copy-start.6 = (s32[8,128]{1,0:T(8,128)S(1)}, s32[8,128]{1,0:T(8,128)}, u32[]{:S(2)}) copy-start(s32[8,128]{1,0:T(8,128)} %refs_0_.1) | copy-start | bytes 12292
  2.9 20.2 %copy-start.4 = (f32[8,2048]{1,0:T(8,128)S(1)}, f32[8,2048]{1,0:T(8,128)}, u32[]{:S(2)}) copy-start(f32[8,2048]{1,0:T(8,128)} %get-tuple-element.22.source_ref) | copy-start | bytes 196612
  2.9 33.5 %all-to-all-start = ((f32[128,7,1,128]{3,2,1,0:T(1,128)}), f32[128,7,1,128]{3,2,1,0:T(1,128)S(1)}, u32[]{:S(2)}, u32[]{:S(2)}) async-start(f32[128,7,1,128]{3,2,1,0:T(1,128)} %bitcast.7), calls=%async_computation | async-start | bytes 917504 | tf_op jit(solution)/shard_map/all_to_all | solution.py:419
  19.3 4.7 %collective-permute-start = (s32[64,128]{1,0:T(8,128)}, s32[64,128]{1,0:T(8,128)S(1)}, u32[]{:S(2)}, u32[]{:S(2)}) collective-permute-start(s32[64,128]{1,0:T(8,128)} %get-tuple-element.25.here_ref), channel_id=1, source_target_pairs={{0,1},{1,0},{2,3},{3,2},{4,5},{5,4},{6,7},{7,6},{8,9},{9,8},{10,11... | collective-permute-start | bytes 98312 | tf_op jit(solution)/shard_map/ppermute | solution.py:415
  20.6 0.7 copy-start.5
  23.6 0.5 copy-start.8
  24.1 43.5 %copy-start.9 = (s32[1,128]{1,0:T(1,128)S(1)}, s32[1,128]{1,0:T(1,128)}, u32[]{:S(2)}) copy-start(s32[1,128]{1,0:T(1,128)} %copy-done.8) | copy-start | bytes 1540
  44.1 29.3 %copy-start = (f32[3,2048]{1,0:T(4,128)S(1)}, f32[3,2048]{1,0:T(4,128)}, u32[]{:S(2)}) copy-start(f32[3,2048]{1,0:T(4,128)} %pos_ref.3) | copy-start | bytes 73732
  44.1 29.3 %copy-start.1 = (f32[3,2048]{1,0:T(4,128)S(1)}, f32[3,2048]{1,0:T(4,128)}, u32[]{:S(2)}) copy-start(f32[3,2048]{1,0:T(4,128)} %vel_ref.3) | copy-start | bytes 73732
  44.2 29.3 %copy-start.2 = (f32[3,2048]{1,0:T(4,128)S(1)}, f32[3,2048]{1,0:T(4,128)}, u32[]{:S(2)}) copy-start(f32[3,2048]{1,0:T(4,128)} %acc_ref.3) | copy-start | bytes 73732
  44.2 29.3 %copy-start.3 = (f32[3,2048]{1,0:T(4,128)S(1)}, f32[3,2048]{1,0:T(4,128)}, u32[]{:S(2)}) copy-start(f32[3,2048]{1,0:T(4,128)} %jrk_ref.3) | copy-start | bytes 73732
  44.2 29.3 %copy-start.7 = (s32[64,128]{1,0:T(8,128)S(1)}, s32[64,128]{1,0:T(8,128)}, u32[]{:S(2)}) copy-start(s32[64,128]{1,0:T(8,128)} %get-tuple-element.25.here_ref) | copy-start | bytes 98308
  68.2 5.3 %collective-permute-start.1 = (f32[16,128]{1,0:T(8,128)S(1)}, f32[16,128]{1,0:T(8,128)S(1)}, u32[]{:S(2)}, u32[]{:S(2)}) collective-permute-start(f32[16,128]{1,0:T(8,128)S(1)} %get-tuple-element.31.mine_ref), channel_id=1, source_target_pairs={{0,1},{1,0},{2,3},{3,2},{4,5},{5,4},{6,7},{7,6},{8,9},{9,8},{10,11... | collective-permute-start | bytes 24584 | tf_op jit(solution)/shard_map/ppermute | solution.py:415

commit v4 on v3

--- a/solution.py
+++ b/solution.py
@@ -11,6 +11,7 @@
 ROWS = 7
 LANES = 128
 PLANE = ("y", "x")
+PLANE_SIZE = 16
 SRC = ("z", "y", "x")
 F32 = jnp.float32
 BF16 = jnp.bfloat16
@@ -54,19 +55,16 @@
     return lax.broadcasted_iota(jnp.int32, shape, axis)
 
 
-def pick_kernel(me_ref, pos_ref, vel_ref, acc_ref, jrk_ref, mass_ref, phase_ref, level_ref, active_ref,
-                send_ref, source_ref, place_ref):
-    count = pos_ref.shape[1]
+def pick_kernel(me_ref, active_hbm, *refs):
+    inputs, send_ref, source_ref, place_ref = refs[0:7], refs[7], refs[8], refs[9]
+    active_ref, kept, arrived = refs[10], refs[11:18], refs[18]
+    copies = [pltpu.make_async_copy(active_hbm, active_ref, arrived.at[7])]
+    copies += [pltpu.make_async_copy(here, there, arrived.at[i]) for i, (here, there) in enumerate(zip(inputs, kept))]
+    for copy in copies:
+        copy.start()
+    count = kept[0].shape[1]
     rows = active_ref.shape[0]
-    position, velocity = pos_ref[...], vel_ref[...]
-    accel, jerk = acc_ref[...], jrk_ref[...]
-    tau = phase_ref[...] * jnp.exp2(-level_ref[...].astype(F32))
-    pred_x = position + tau * (velocity + tau * (accel * 0.5 + tau * (jerk / 6.0)))
-    pred_v = velocity + tau * (accel + tau * (jerk * 0.5))
-    base_x = pred_x - tau * tau * (0.15 * accel + tau * (jerk * (7.0 / 60.0)))
-    base_v = pred_v - tau * (0.5 * accel + tau * (jerk * (5.0 / 12.0)))
-    source_ref[...] = jnp.concatenate([pred_x, pred_v, mass_ref[...], tau], axis=0)
-
+    copies[0].wait()
     offset = active_ref[...] - me_ref[0] * count
     owned = (offset >= 0) & (offset < count)
     flag = jnp.where(owned, 1.0, 0.0)
@@ -83,32 +81,43 @@
         running = running + totals[row:row + 1]
     spot = jnp.sum(place.astype(F32), axis=1, keepdims=True).astype(jnp.int32) - 1
     place_ref[...] = jnp.broadcast_to(spot, (SLOTS, LANES))
-
+    onehot = jnp.where(iota((SLOTS, count), 1) == spot, 1.0, 0.0).astype(BF16)
+
+    for copy in copies[1:]:
+        copy.wait()
+    position, velocity, accel, jerk, mass, phase, level = [ref[...] for ref in kept]
+    tau = phase * jnp.exp2(-level.astype(F32))
+    pred_x = position + tau * (velocity + tau * (accel * 0.5 + tau * (jerk / 6.0)))
+    pred_v = velocity + tau * (accel + tau * (jerk * 0.5))
+    base_x = pred_x - tau * tau * (0.15 * accel + tau * (jerk * (7.0 / 60.0)))
+    base_v = pred_v - tau * (0.5 * accel + tau * (jerk * (5.0 / 12.0)))
+    source_ref[...] = jnp.concatenate([pred_x, pred_v, mass, tau], axis=0)
     table = jnp.concatenate([pred_x, pred_v, tau, tau, base_x, base_v, tau, tau], axis=0)
-    onehot = jnp.where(iota((SLOTS, count), 1) == spot, 1.0, 0.0).astype(BF16)
     terms = jnp.concatenate(three_terms(table), axis=0)
     picked = lax.dot_general(terms, onehot, (((1,), (1,)), ((), ())), preferred_element_type=F32)
     picked = picked[0:16] + picked[16:32] + picked[32:48]
     block = jnp.concatenate([picked[0:8], picked[8:16]], axis=1)[0:ROWS]
-    blocks = jnp.concatenate([block] * 8, axis=0)
-    for piece in range(send_ref.shape[0] // (8 * ROWS)):
-        send_ref[piece * 8 * ROWS:(piece + 1) * 8 * ROWS] = blocks
-
-
-def pick(me, position, velocity, accel, jerk_old, masses, phase, levels, active, owners):
+    blocks = jnp.concatenate([block] * (send_ref.shape[0] // ROWS), axis=0)
+    send_ref[...] = blocks
+
+
+def pick(me, position, velocity, accel, jerk_old, masses, phase, levels, active, peers):
     count = position.shape[1]
+    inputs = (position, velocity, accel, jerk_old, masses, phase, levels)
     return pl.pallas_call(
         pick_kernel,
         out_shape=(
-            jax.ShapeDtypeStruct((owners * ROWS, LANES), F32),
+            jax.ShapeDtypeStruct((peers * ROWS, LANES), F32),
             jax.ShapeDtypeStruct((8, count), F32),
             jax.ShapeDtypeStruct((SLOTS, LANES), jnp.int32),
         ),
-        in_specs=[smem()] + [vmem()] * 8,
+        in_specs=[smem()] + [hbm()] * 8,
         out_specs=(vmem(), vmem(), vmem()),
-        compiler_params=params(56),
+        scratch_shapes=[pltpu.VMEM(value.shape, value.dtype) for value in (active,) + inputs]
+        + [pltpu.SemaphoreType.DMA((8,))],
+        compiler_params=params(8),
         name="pick",
-    )(me, position, velocity, accel, jerk_old, masses, phase, levels, active)
+    )(me, pinned(active), *[pinned(value) for value in inputs])
 
 
 def sort_keys(active, count):
@@ -117,7 +126,7 @@
     return (owner * (rows * LANES) + iota((rows, LANES), 0) * LANES + iota((rows, LANES), 1)).astype(F32)
 
 
-def prepare_kernel(source_ref, active_ref, first_ref, factor_ref, moment_ref):
+def prepare_kernel(source_ref, active_ref, first_hbm, factor_ref, moment_ref, perm_ref, first_ref, sent):
     count = source_ref.shape[1]
     rows = active_ref.shape[0]
     total = rows * LANES
@@ -125,10 +134,20 @@
     columns = jnp.transpose(key)
     limit = (iota((1, LANES), 1) * total).astype(F32)
     first = jnp.zeros((8, LANES), F32)
+    ranks = [jnp.zeros((8, LANES), F32) for _ in range(rows)]
     for row in range(rows):
         column = jnp.broadcast_to(columns[:, row:row + 1], (LANES, LANES))
         first = first + jnp.sum(jnp.where(column < limit, 1.0, 0.0).reshape(LANES // 8, 8, LANES), axis=0)
+        for to in range(rows):
+            less = jnp.where(column < key[to:to + 1], 1.0, 0.0)
+            ranks[to] = ranks[to] + jnp.sum(less.reshape(LANES // 8, 8, LANES), axis=0)
     first_ref[...] = jnp.sum(first, axis=0, keepdims=True).astype(jnp.int32)
+    copy = pltpu.make_async_copy(first_ref, first_hbm, sent)
+    copy.start()
+    spots = iota((total, LANES), 0)
+    for to in range(rows):
+        rank = jnp.sum(ranks[to], axis=0, keepdims=True).astype(jnp.int32)
+        perm_ref[:, to * LANES:(to + 1) * LANES] = jnp.where(spots == rank, 1.0, 0.0).astype(BF16)
 
     source = source_ref[...]
     terms = [term.astype(F32) for term in three_terms(source)]
@@ -145,20 +164,24 @@
         here = slice(piece * LANES, (piece + 1) * LANES)
         across = jnp.transpose(stack[:, here])
         factor_ref[here, :] = jnp.concatenate([across, jnp.zeros((LANES, LANES - 56), F32)], axis=1).astype(BF16)
+    copy.wait()
 
 
 def prepare(source, active):
     count = source.shape[1]
+    total = active.shape[0] * LANES
     return pl.pallas_call(
         prepare_kernel,
         out_shape=(
             jax.ShapeDtypeStruct((1, LANES), jnp.int32),
             jax.ShapeDtypeStruct((count, LANES), BF16),
             jax.ShapeDtypeStruct((32, count), BF16),
+            jax.ShapeDtypeStruct((total, total), BF16),
         ),
         in_specs=[vmem()] * 2,
-        out_specs=(vmem(),) * 3,
-        compiler_params=params(PREP),
+        out_specs=(hbm(),) + (vmem(),) * 3,
+        scratch_shapes=[pltpu.VMEM((1, LANES), jnp.int32), pltpu.SemaphoreType.DMA],
+        compiler_params=params(12),
         cost_estimate=cost(5),
         name="prepare",
     )(source, active)
@@ -168,7 +191,8 @@
     start = first_ref[0, owner]
     block = lax.shift_right_logical(start, 7)
     shift = lax.bitwise_and(start, LANES - 1)
-    low = owner * ROWS
+    depth = states_ref.shape[0] // ROWS // PLANE_SIZE
+    low = (owner % PLANE_SIZE * depth + owner // PLANE_SIZE) * ROWS
     if low + 8 <= states_ref.shape[0]:
         value = states_ref[low:low + 8]
     else:
@@ -176,36 +200,6 @@
     turned = pltpu.roll(value, lax.bitwise_and(shift + half * SLOTS, LANES - 1), 1)
     pltpu.store(compact.at[block], turned, mask=iota((8, LANES), 1) >= shift)
     compact[block + 1] = turned
-
-
-def tables_kernel(count, active_ref, perm_ref):
-    rows = active_ref.shape[0]
-    total = rows * LANES
-    key = sort_keys(active_ref[...], count)
-    columns = jnp.transpose(key)
-    ranks = [jnp.zeros((8, LANES), F32) for _ in range(rows)]
-    for row in range(rows):
-        column = jnp.broadcast_to(columns[:, row:row + 1], (LANES, LANES))
-        for to in range(rows):
-            less = jnp.where(column < key[to:to + 1], 1.0, 0.0)
-            ranks[to] = ranks[to] + jnp.sum(less.reshape(LANES // 8, 8, LANES), axis=0)
-    spots = iota((total, LANES), 0)
-    for to in range(rows):
-        rank = jnp.sum(ranks[to], axis=0, keepdims=True).astype(jnp.int32)
-        perm_ref[:, to * LANES:(to + 1) * LANES] = jnp.where(spots == rank, 1.0, 0.0).astype(BF16)
-
-
-def tables(active, count):
-    total = active.shape[0] * LANES
-    return pl.pallas_call(
-        lambda *refs: tables_kernel(count, *refs),
-        out_shape=jax.ShapeDtypeStruct((total, total), BF16),
-        in_specs=[vmem()],
-        out_specs=vmem(),
-        compiler_params=params(8),
-        cost_estimate=cost(4),
-        name="tables",
-    )(active)
 
 
 def force_kernel(first_hbm, states_ref, factor_ref, moment_ref, send_ref, state_ref,
@@ -308,6 +302,21 @@
     )(pinned(first), states, factor, moment)
 
 
+def repeat_kernel(value_ref, send_ref):
+    send_ref[...] = jnp.broadcast_to(value_ref[...][None], send_ref.shape)
+
+
+def repeat(value, peers):
+    return pl.pallas_call(
+        repeat_kernel,
+        out_shape=jax.ShapeDtypeStruct((peers,) + value.shape, F32),
+        in_specs=[vmem()],
+        out_specs=vmem(),
+        compiler_params=params(4),
+        name="repeat",
+    )(value)
+
+
 def add_kernel(parts_ref, send_ref):
     total = jnp.sum(parts_ref[...], axis=0)
     send_ref[...] = jnp.broadcast_to(total[None], send_ref.shape)
@@ -425,13 +434,13 @@
     me = lax.axis_index(SRC).reshape(1).astype(jnp.int32)
     send, source, mine = pick(
         me, position, velocity, accel, jerk_old, masses.reshape(1, count), phase.reshape(1, count),
-        levels.reshape(1, count), active, owners,
+        levels.reshape(1, count), active, depth,
     )
-    states = exchange(send.reshape(owners, ROWS, 1, LANES), SRC).reshape(send.shape)
+    column = exchange(send.reshape(depth, ROWS, 1, LANES), "z").reshape(send.shape)
     other = swap(mine)
-    first, factor, moment = prepare(source, active)
-    perm = tables(active, count)
-    states, other, perm = lax.optimization_barrier((states, other, perm))
+    first, factor, moment, perm = prepare(source, active)
+    column, other, perm, factor = lax.optimization_barrier((column, other, perm, factor))
+    states = exchange(repeat(column, plane), PLANE).reshape(owners * ROWS, LANES)
     send, state = forces(first, states, factor, moment, blocks, plane)
     parts = exchange(add_parts(exchange(send, PLANE), depth), "z")
     own, wide = correct(me, first, parts, state)
@@ -442,7 +451,7 @@
 
 def solution(mesh):
     owners = mesh.shape["src"]
-    plane = 16
+    plane = PLANE_SIZE
     depth = owners // plane
     fine = Mesh(mesh.devices.reshape(depth, 4, 4, mesh.shape["act"]), ("z", "y", "x", "core"))
     stars = P(None, SRC)

time: 74.9 us -> 74.7 us (level)
  blocking collectives: 23.3 us -> 41.7 us
  waiting for transfers between devices: 12.3 us -> 2.6 us
  starting transfers between devices: 21.9 us -> 13.6 us
    all_to_all x2 -> x3, blocking collectives: 23.3 us -> 41.7 us  [exchange(): return lax.all_to_all(value, axes, 0, 0, tiled=True)]
    all_to_all x1, waiting for transfers between devices: 12.3 us -> 2.6 us  [exchange(): return lax.all_to_all(value, axes, 0, 0, tiled=True)]
    all_to_all x1, starting transfers between devices: 16.5 us -> 9.03 us  [exchange(): return lax.all_to_all(value, axes, 0, 0, tiled=True)]
    pallas_call x2, Pallas kernels: 3.99 us -> 2.06 us  [the longest x1 2.03 us: pick(): pl.pallas_call(pick_kernel, out_shape=(jax.ShapeDtypeStruct((peers * ROWS...]
    pallas_call x1, Pallas kernels: 0.49 us -> 2.07 us  [prepare(): pl.pallas_call(prepare_kernel, out_shape=(jax.ShapeDtypeStruct((1, LANES)...]
    ppermute x2, starting transfers between devices: 5.42 us -> 4.53 us  [swap(): return lax.ppermute(value, 'core', [(0, 1), (1, 0)])]
  transfers between devices with their start and end apart: 3 -> 3, of which waited for: 1 -> 1; matrix products, arithmetic and copies ran while one was open for 0% -> 0% of each run, Pallas kernels for 5% -> 4%
where the time goes in v4:
time: 74.7 us; the launch traced here: 74.3 us
  blocking collectives  41.7 us (56%)
  Pallas kernels  14.4 us (19%)
  starting transfers between devices  13.6 us (18%)
  waiting for transfers between devices  2.6 us (3%)
  local copies, waits for them, and re-layouts  1.22 us (2%)
    all_to_all x3, blocking collectives, exchange(): return lax.all_to_all(value, axes, 0, 0, tiled=True)  41.7 us
    all_to_all x1, starting transfers between devices, exchange(): return lax.all_to_all(value, axes, 0, 0, tiled=True)  9.03 us
    pallas_call x1, Pallas kernels, forces(): pl.pallas_call(force_kernel, out_shape=(jax.ShapeDtypeStruct((peers, 6 *...  7.62 us
    ppermute x2, starting transfers between devices, swap(): return lax.ppermute(value, 'core', [(0, 1), (1, 0)])  4.53 us
    all_to_all x1, waiting for transfers between devices, exchange(): return lax.all_to_all(value, axes, 0, 0, tiled=True)  2.6 us
    pallas_call x1, Pallas kernels, prepare(): pl.pallas_call(prepare_kernel, out_shape=(jax.ShapeDtypeStruct((1, LANES)...  2.07 us
    pallas_call x1, Pallas kernels, pick(): pl.pallas_call(pick_kernel, out_shape=(jax.ShapeDtypeStruct((peers * ROWS...  2.03 us
  transfers between devices with their start and end apart: 3, of which 1 were waited for; matrix products, arithmetic and copies ran while one was open for 0% of the time, Pallas kernels for 4%

profile of v4, /device:TPU:1, one launch (start us, length us, event | category | flops | bytes accessed | tf_op | source)
XLA Modules:
  0.0 74.3 jit_solution(12957893281133842161)
XLA Ops:
  0.6 2.0 %pick.1 = (f32[56,128]{1,0:T(8,128)}, f32[8,2048]{1,0:T(8,128)S(1)}, s32[64,128]{1,0:T(8,128)S(1)}) custom-call(s32[1]{0:T(128)} %bitcast.me_ref, s32[8,128]{1,0:T(8,128)} %active_ref.1, f32[3,2048]{1,0:T(4,128)} %pos_ref.1, f32[3,2048]{1,0:T(4,128)} %vel_ref.1, f32[3,2048]{1,0:T(4,128)} %acc_ref.1, f32[3,2048]{1,0:T(4,128)} %jrk_ref.1, f32[1,2048]{1,0:T(1,128)} %bitcast.9, ...), custom_call_target="tpu_custom_call" | custom-call | tf_op jit(solution)/shard_map/pick/pallas_call | solution.py:107
  2.7 9.0 %all-to-all-start = ((f32[8,7,1,128]{3,2,1,0:T(1,128)}), f32[8,7,1,128]{3,2,1,0:T(1,128)S(1)}, u32[]{:S(2)}, u32[]{:S(2)}) async-start(f32[8,7,1,128]{3,2,1,0:T(1,128)} %bitcast.4), calls=%async_computation | async-start | bytes 57344 | tf_op jit(solution)/shard_map/all_to_all | solution.py:428
  11.7 1.0 %collective-permute-start = (s32[64,128]{1,0:T(8,128)S(1)}, s32[64,128]{1,0:T(8,128)S(1)}, u32[]{:S(2)}, u32[]{:S(2)}) collective-permute-start(s32[64,128]{1,0:T(8,128)S(1)} %get-tuple-element.27.here_ref), channel_id=1, source_target_pairs={{0,1},{1,0},{2,3},{3,2},{4,5},{5,4},{6,7},{7,6},{8,9},{9,8},{10,11... | collective-permute-start | bytes 98312 | tf_op jit(solution)/shard_map/ppermute | solution.py:424
  12.7 0.0 copy-start.4
  12.7 0.7 copy-done.4
  13.3 2.1 %prepare.1 = (s32[1,128]{1,0:T(1,128)S(1)}, bf16[2048,128]{1,0:T(8,128)(2,1)S(1)}, bf16[32,2048]{1,0:T(8,128)(2,1)S(1)}, bf16[1024,1024]{1,0:T(8,128)(2,1)S(1)}) custom-call(f32[8,2048]{1,0:T(8,128)S(1)} %get-tuple-element.24.source_ref, s32[8,128]{1,0:T(8,128)S(1)} %copy-done.4), custom_call_target="tpu_custom_call" | custom-call | bytes 15000000 | tf_op jit(solution)/shard_map/prepare/pallas_call | solution.py:173
  15.4 0.0 copy-start.5
  15.4 0.5 copy-done.5
  15.9 0.0 collective-permute-done.there_ref
  15.9 2.6 %all-to-all-done = f32[8,7,1,128]{3,2,1,0:T(1,128)S(1)} async-done(((f32[8,7,1,128]{3,2,1,0:T(1,128)}), f32[8,7,1,128]{3,2,1,0:T(1,128)S(1)}, u32[]{:S(2)}, u32[]{:S(2)}) %all-to-all-start) | async-done | bytes 28704 | tf_op jit(solution)/shard_map/all_to_all | solution.py:428
  18.5 0.0 copy-start.6
  18.6 15.3 %all_to_all.20 = f32[16,56,128]{2,1,0:T(8,128)S(1)} all-to-all(f32[16,56,128]{2,1,0:T(8,128)S(1)} %repeat.1), channel_id=1, replica_groups=mesh['z'=8,'y'=4,'x'=4,'core'=2] {'y','x'}, dimensions={0} | all-to-all | bytes 917504 | tf_op jit(solution)/shard_map/all_to_all | solution.py:428
  33.9 7.6 %forces.1 = (f32[16,48,128]{2,1,0:T(8,128)S(1)}, f32[8,8,128]{2,1,0:T(8,128)S(1)}) custom-call(s32[1,128]{1,0:T(1,128)} %copy-done.5, f32[896,128]{1,0:T(8,128)S(1)} %bitcast.7, bf16[2048,128]{1,0:T(8,128)(2,1)S(1)} %get-tuple-element.31.factor_ref, bf16[32,2048]{1,0:T(8,128)(2,1)S(1)} %get-tuple-element.32.moment_ref), custom_call_target="tpu_custom_call" | custom-call | bytes 27000000 | tf_op jit(solution)/shard_map/forces/pallas_call | solution.py:284
  41.5 0.0 copy-start
  41.6 0.0 copy-start.1
  41.6 0.0 copy-start.2
  41.6 0.0 copy-start.3
  41.6 11.1 %all_to_all.21.parts_ref = f32[16,48,128]{2,1,0:T(8,128)S(1)} all-to-all(f32[16,48,128]{2,1,0:T(8,128)S(1)} %get-tuple-element.33), channel_id=1, replica_groups=mesh['z'=8,'y'=4,'x'=4,'core'=2] {'y','x'}, dimensions={0} | all-to-all | bytes 786432 | tf_op jit(solution)/shard_map/all_to_all | solution.py:428
  52.7 15.3 %all_to_all.22.parts_ref = f32[8,48,128]{2,1,0:T(8,128)S(1)} all-to-all(f32[8,48,128]{2,1,0:T(8,128)S(1)} %add_parts.1), channel_id=1, replica_groups=mesh['z'=8,'y'=4,'x'=4,'core'=2] {'z'}, dimensions={0} | all-to-all | bytes 393216 | tf_op jit(solution)/shard_map/all_to_all | solution.py:428
  68.0 0.0 copy-done.6
  68.0 0.6 correct.1
  68.7 3.6 %collective-permute-start.1 = (f32[16,128]{1,0:T(8,128)S(1)}, f32[16,128]{1,0:T(8,128)S(1)}, u32[]{:S(2)}, u32[]{:S(2)}) collective-permute-start(f32[16,128]{1,0:T(8,128)S(1)} %get-tuple-element.35.mine_ref), channel_id=1, source_target_pairs={{0,1},{1,0},{2,3},{3,2},{4,5},{5,4},{6,7},{7,6},{8,9},{9,8},{10,11... | collective-permute-start | bytes 24584 | tf_op jit(solution)/shard_map/ppermute | solution.py:424
  72.2 1.1 %permute.1 = f32[12,1024]{1,0:T(8,128)} custom-call(f32[16,10,128]{2,1,0:T(8,128)S(1)} %get-tuple-element.41.wide_ref, bf16[1024,1024]{1,0:T(8,128)(2,1)S(1)} %get-tuple-element.42.perm_ref), custom_call_target="tpu_custom_call" | custom-call | bytes 6000000 | tf_op jit(solution)/shard_map/permute/pallas_call | solution.py:385
  73.3 0.0 collective-permute-done.1.other_ref
  73.3 0.0 copy-done
  73.3 0.0 copy-done.1
  73.3 0.0 copy-done.2
  73.3 0.0 copy-done.3
  73.3 0.9 %write.1 = (f32[3,2048]{1,0:T(4,128)}, f32[3,2048]{1,0:T(4,128)}, f32[3,2048]{1,0:T(4,128)}, f32[3,2048]{1,0:T(4,128)}) custom-call(f32[16,128]{1,0:T(8,128)S(1)} %get-tuple-element.35.mine_ref, f32[16,128]{1,0:T(8,128)S(1)} %collective-permute-done.1.other_ref, s32[64,128]{1,0:T(8,128)S(1)} %get-tuple-element.27.here_ref, ...), custom_call_target="tpu_custom_call" | custom-call | tf_op jit(solution)/shard_map/write/pallas_call | solution.py:413
  (2 shorter events, 0.1 us)
Async XLA Ops:
  2.7 15.9 %all-to-all-start = ((f32[8,7,1,128]{3,2,1,0:T(1,128)}), f32[8,7,1,128]{3,2,1,0:T(1,128)S(1)}, u32[]{:S(2)}, u32[]{:S(2)}) async-start(f32[8,7,1,128]{3,2,1,0:T(1,128)} %bitcast.4), calls=%async_computation | async-start | bytes 57344 | tf_op jit(solution)/shard_map/all_to_all | solution.py:428
  11.7 4.2 %collective-permute-start = (s32[64,128]{1,0:T(8,128)S(1)}, s32[64,128]{1,0:T(8,128)S(1)}, u32[]{:S(2)}, u32[]{:S(2)}) collective-permute-start(s32[64,128]{1,0:T(8,128)S(1)} %get-tuple-element.27.here_ref), channel_id=1, source_target_pairs={{0,1},{1,0},{2,3},{3,2},{4,5},{5,4},{6,7},{7,6},{8,9},{9,8},{10,11... | collective-permute-start | bytes 98312 | tf_op jit(solution)/shard_map/ppermute | solution.py:424
  12.7 0.7 copy-start.4
  15.4 0.5 copy-start.5
  18.5 49.5 %copy-start.6 = (s32[1,128]{1,0:T(1,128)S(1)}, s32[1,128]{1,0:T(1,128)}, u32[]{:S(2)}) copy-start(s32[1,128]{1,0:T(1,128)} %copy-done.5) | copy-start | bytes 1540
  41.5 31.8 %copy-start = (f32[3,2048]{1,0:T(4,128)S(1)}, f32[3,2048]{1,0:T(4,128)}, u32[]{:S(2)}) copy-start(f32[3,2048]{1,0:T(4,128)} %pos_ref.1) | copy-start | bytes 73732
  41.6 31.8 %copy-start.1 = (f32[3,2048]{1,0:T(4,128)S(1)}, f32[3,2048]{1,0:T(4,128)}, u32[]{:S(2)}) copy-start(f32[3,2048]{1,0:T(4,128)} %vel_ref.1) | copy-start | bytes 73732
  41.6 31.8 %copy-start.2 = (f32[3,2048]{1,0:T(4,128)S(1)}, f32[3,2048]{1,0:T(4,128)}, u32[]{:S(2)}) copy-start(f32[3,2048]{1,0:T(4,128)} %acc_ref.1) | copy-start | bytes 73732
  41.6 31.8 %copy-start.3 = (f32[3,2048]{1,0:T(4,128)S(1)}, f32[3,2048]{1,0:T(4,128)}, u32[]{:S(2)}) copy-start(f32[3,2048]{1,0:T(4,128)} %jrk_ref.1) | copy-start | bytes 73732
  68.7 4.7 %collective-permute-start.1 = (f32[16,128]{1,0:T(8,128)S(1)}, f32[16,128]{1,0:T(8,128)S(1)}, u32[]{:S(2)}, u32[]{:S(2)}) collective-permute-start(f32[16,128]{1,0:T(8,128)S(1)} %get-tuple-element.35.mine_ref), channel_id=1, source_target_pairs={{0,1},{1,0},{2,3},{3,2},{4,5},{5,4},{6,7},{7,6},{8,9},{9,8},{10,11... | collective-permute-start | bytes 24584 | tf_op jit(solution)/shard_map/ppermute | solution.py:424

commit v5 on v4

--- a/solution.py
+++ b/solution.py
@@ -437,10 +437,11 @@
         levels.reshape(1, count), active, depth,
     )
     column = exchange(send.reshape(depth, ROWS, 1, LANES), "z").reshape(send.shape)
+    column, late, mine = lax.optimization_barrier((column, active, mine))
+    states = exchange(repeat(column, plane), PLANE).reshape(owners * ROWS, LANES)
     other = swap(mine)
-    first, factor, moment, perm = prepare(source, active)
-    column, other, perm, factor = lax.optimization_barrier((column, other, perm, factor))
-    states = exchange(repeat(column, plane), PLANE).reshape(owners * ROWS, LANES)
+    first, factor, moment, perm = prepare(source, late)
+    states, other, perm = lax.optimization_barrier((states, other, perm))
     send, state = forces(first, states, factor, moment, blocks, plane)
     parts = exchange(add_parts(exchange(send, PLANE), depth), "z")
     own, wide = correct(me, first, parts, state)

time: 74.7 us -> 72.9 us (0.976)
  blocking collectives: 41.7 us -> 38.8 us
    all_to_all x3, blocking collectives: 41.7 us -> 38.8 us  [exchange(): return lax.all_to_all(value, axes, 0, 0, tiled=True)]
    ppermute x2, starting transfers between devices: 4.53 us -> 7.33 us  [swap(): return lax.ppermute(value, 'core', [(0, 1), (1, 0)])]
    all_to_all x1, starting transfers between devices: 9.03 us -> 6.75 us  [exchange(): return lax.all_to_all(value, axes, 0, 0, tiled=True)]
    pallas_call x1, Pallas kernels: 0.03 us -> 0.79 us  [repeat(): pl.pallas_call(repeat_kernel, out_shape=jax.ShapeDtypeStruct((peers,) + v...]
where the time goes in v5:
time: 72.9 us; the launch traced here: 72.5 us
  blocking collectives  38.8 us (53%)
  Pallas kernels  14.6 us (20%)
  starting transfers between devices  14.1 us (19%)
  waiting for transfers between devices  3.03 us (4%)
  local copies, waits for them, and re-layouts  1.22 us (2%)
  between operations  0.74 us (1%)
    all_to_all x3, blocking collectives, exchange(): return lax.all_to_all(value, axes, 0, 0, tiled=True)  38.8 us
    pallas_call x1, Pallas kernels, forces(): pl.pallas_call(force_kernel, out_shape=(jax.ShapeDtypeStruct((peers, 6 *...  7.62 us
    ppermute x2, starting transfers between devices, swap(): return lax.ppermute(value, 'core', [(0, 1), (1, 0)])  7.33 us
    all_to_all x1, starting transfers between devices, exchange(): return lax.all_to_all(value, axes, 0, 0, tiled=True)  6.75 us
    all_to_all x1, waiting for transfers between devices, exchange(): return lax.all_to_all(value, axes, 0, 0, tiled=True)  3.03 us
    pallas_call x1, Pallas kernels, prepare(): pl.pallas_call(prepare_kernel, out_shape=(jax.ShapeDtypeStruct((1, LANES)...  2.07 us
  transfers between devices with their start and end apart: 3, of which 1 were waited for; matrix products, arithmetic and copies ran while one was open for 0% of the time, Pallas kernels for 4%

profile of v5, /device:TPU:1, one launch (start us, length us, event | category | flops | bytes accessed | tf_op | source)
XLA Modules:
  0.0 72.5 jit_solution(6913184786560651294)
XLA Ops:
  0.6 1.4 %pick.1 = (f32[56,128]{1,0:T(8,128)S(1)}, f32[8,2048]{1,0:T(8,128)S(1)}, s32[64,128]{1,0:T(8,128)S(1)}) custom-call(s32[1]{0:T(128)} %bitcast.me_ref, s32[8,128]{1,0:T(8,128)} %active_ref, f32[3,2048]{1,0:T(4,128)} %pos_ref.1, f32[3,2048]{1,0:T(4,128)} %vel_ref.1, f32[3,2048]{1,0:T(4,128)} %acc_ref.1, f32[3,2048]{1,0:T(4,128)} %jrk_ref.1, ...), custom_call_target="tpu_custom_call" | custom-call | tf_op jit(solution)/shard_map/pick/pallas_call | solution.py:107
  2.1 15.6 %all_to_all.20 = f32[8,7,1,128]{3,2,1,0:T(1,128)S(1)} all-to-all(f32[8,7,1,128]{3,2,1,0:T(1,128)S(1)} %bitcast.9), channel_id=1, replica_groups=mesh['z'=8,'y'=4,'x'=4,'core'=2] {'z'}, dimensions={0} | all-to-all | bytes 57344 | tf_op jit(solution)/shard_map/all_to_all | solution.py:428
  17.7 0.8 %repeat.1 = f32[16,56,128]{2,1,0:T(8,128)} custom-call(f32[56,128]{1,0:T(8,128)S(1)} %bitcast.8), custom_call_target="tpu_custom_call" | custom-call | tf_op jit(solution)/shard_map/repeat/pallas_call | solution.py:310
  18.5 6.8 %all-to-all-start.1 = ((f32[16,56,128]{2,1,0:T(8,128)}), f32[16,56,128]{2,1,0:T(8,128)S(1)}, u32[]{:S(2)}, u32[]{:S(2)}) async-start(f32[16,56,128]{2,1,0:T(8,128)} %repeat.1), calls=%async_computation.1 | async-start | bytes 917504 | tf_op jit(solution)/shard_map/all_to_all | solution.py:428
  25.3 2.5 %collective-permute-start = (s32[64,128]{1,0:T(8,128)S(1)}, s32[64,128]{1,0:T(8,128)S(1)}, u32[]{:S(2)}, u32[]{:S(2)}) collective-permute-start(s32[64,128]{1,0:T(8,128)S(1)} %get-tuple-element.32.here_ref), channel_id=1, source_target_pairs={{0,1},{1,0},{2,3},{3,2},{4,5},{5,4},{6,7},{7,6},{8,9},{9,8},{10,11... | collective-permute-start | bytes 98312 | tf_op jit(solution)/shard_map/ppermute | solution.py:424
  27.7 0.0 copy-start.4
  27.7 0.7 copy-done.4
  28.4 2.1 %prepare.1 = (s32[1,128]{1,0:T(1,128)S(1)}, bf16[2048,128]{1,0:T(8,128)(2,1)S(1)}, bf16[32,2048]{1,0:T(8,128)(2,1)S(1)}, bf16[1024,1024]{1,0:T(8,128)(2,1)S(1)}) custom-call(f32[8,2048]{1,0:T(8,128)S(1)} %get-tuple-element.26.source_ref, s32[8,128]{1,0:T(8,128)S(1)} %copy-done.4), custom_call_target="tpu_custom_call" | custom-call | bytes 15000000 | tf_op jit(solution)/shard_map/prepare/pallas_call | solution.py:173
  30.5 0.0 copy-start.5
  30.5 0.5 copy-done.5
  31.0 0.0 collective-permute-done.there_ref
  31.0 0.0 copy-start.6
  31.0 3.0 %all-to-all-done.1 = f32[16,56,128]{2,1,0:T(8,128)S(1)} async-done(((f32[16,56,128]{2,1,0:T(8,128)}), f32[16,56,128]{2,1,0:T(8,128)S(1)}, u32[]{:S(2)}, u32[]{:S(2)}) %all-to-all-start.1) | async-done | bytes 458784 | tf_op jit(solution)/shard_map/all_to_all | solution.py:428
  34.1 7.6 %forces.1 = (f32[16,48,128]{2,1,0:T(8,128)S(1)}, f32[8,8,128]{2,1,0:T(8,128)S(1)}) custom-call(s32[1,128]{1,0:T(1,128)} %copy-done.5, f32[896,128]{1,0:T(8,128)S(1)} %bitcast.7, bf16[2048,128]{1,0:T(8,128)(2,1)S(1)} %get-tuple-element.35.factor_ref, bf16[32,2048]{1,0:T(8,128)(2,1)S(1)} %get-tuple-element.36.moment_ref), custom_call_target="tpu_custom_call" | custom-call | bytes 27000000 | tf_op jit(solution)/shard_map/forces/pallas_call | solution.py:284
  41.7 0.0 copy-start
  41.7 0.0 copy-start.1
  41.7 0.0 copy-start.2
  41.7 0.0 copy-start.3
  41.7 12.1 %all_to_all.21.parts_ref = f32[16,48,128]{2,1,0:T(8,128)S(1)} all-to-all(f32[16,48,128]{2,1,0:T(8,128)S(1)} %get-tuple-element.37), channel_id=1, replica_groups=mesh['z'=8,'y'=4,'x'=4,'core'=2] {'y','x'}, dimensions={0} | all-to-all | bytes 786432 | tf_op jit(solution)/shard_map/all_to_all | solution.py:428
  53.9 11.0 %all_to_all.22.parts_ref = f32[8,48,128]{2,1,0:T(8,128)S(1)} all-to-all(f32[8,48,128]{2,1,0:T(8,128)S(1)} %add_parts.1), channel_id=1, replica_groups=mesh['z'=8,'y'=4,'x'=4,'core'=2] {'z'}, dimensions={0} | all-to-all | bytes 393216 | tf_op jit(solution)/shard_map/all_to_all | solution.py:428
  64.9 0.0 copy-done.6
  64.9 0.6 correct.1
  65.6 4.9 %collective-permute-start.1 = (f32[16,128]{1,0:T(8,128)S(1)}, f32[16,128]{1,0:T(8,128)S(1)}, u32[]{:S(2)}, u32[]{:S(2)}) collective-permute-start(f32[16,128]{1,0:T(8,128)S(1)} %get-tuple-element.39.mine_ref), channel_id=1, source_target_pairs={{0,1},{1,0},{2,3},{3,2},{4,5},{5,4},{6,7},{7,6},{8,9},{9,8},{10,11... | collective-permute-start | bytes 24584 | tf_op jit(solution)/shard_map/ppermute | solution.py:424
  70.4 1.1 %permute.1 = f32[12,1024]{1,0:T(8,128)} custom-call(f32[16,10,128]{2,1,0:T(8,128)S(1)} %get-tuple-element.45.wide_ref, bf16[1024,1024]{1,0:T(8,128)(2,1)S(1)} %get-tuple-element.46.perm_ref), custom_call_target="tpu_custom_call" | custom-call | bytes 6000000 | tf_op jit(solution)/shard_map/permute/pallas_call | solution.py:385
  71.5 0.0 collective-permute-done.1.other_ref
  71.5 0.0 copy-done
  71.5 0.0 copy-done.1
  71.5 0.0 copy-done.2
  71.5 0.0 copy-done.3
  71.5 0.9 %write.1 = (f32[3,2048]{1,0:T(4,128)}, f32[3,2048]{1,0:T(4,128)}, f32[3,2048]{1,0:T(4,128)}, f32[3,2048]{1,0:T(4,128)}) custom-call(f32[16,128]{1,0:T(8,128)S(1)} %get-tuple-element.39.mine_ref, f32[16,128]{1,0:T(8,128)S(1)} %collective-permute-done.1.other_ref, s32[64,128]{1,0:T(8,128)S(1)} %get-tuple-element.32.here_ref, ...), custom_call_target="tpu_custom_call" | custom-call | tf_op jit(solution)/shard_map/write/pallas_call | solution.py:413
  (1 shorter events, 0.0 us)
Async XLA Ops:
  18.5 15.5 %all-to-all-start.1 = ((f32[16,56,128]{2,1,0:T(8,128)}), f32[16,56,128]{2,1,0:T(8,128)S(1)}, u32[]{:S(2)}, u32[]{:S(2)}) async-start(f32[16,56,128]{2,1,0:T(8,128)} %repeat.1), calls=%async_computation.1 | async-start | bytes 917504 | tf_op jit(solution)/shard_map/all_to_all | solution.py:428
  25.3 5.8 %collective-permute-start = (s32[64,128]{1,0:T(8,128)S(1)}, s32[64,128]{1,0:T(8,128)S(1)}, u32[]{:S(2)}, u32[]{:S(2)}) collective-permute-start(s32[64,128]{1,0:T(8,128)S(1)} %get-tuple-element.32.here_ref), channel_id=1, source_target_pairs={{0,1},{1,0},{2,3},{3,2},{4,5},{5,4},{6,7},{7,6},{8,9},{9,8},{10,11... | collective-permute-start | bytes 98312 | tf_op jit(solution)/shard_map/ppermute | solution.py:424
  27.7 0.7 copy-start.4
  30.5 0.5 copy-start.5
  31.0 33.9 %copy-start.6 = (s32[1,128]{1,0:T(1,128)S(1)}, s32[1,128]{1,0:T(1,128)}, u32[]{:S(2)}) copy-start(s32[1,128]{1,0:T(1,128)} %copy-done.5) | copy-start | bytes 1540
  41.7 29.8 %copy-start = (f32[3,2048]{1,0:T(4,128)S(1)}, f32[3,2048]{1,0:T(4,128)}, u32[]{:S(2)}) copy-start(f32[3,2048]{1,0:T(4,128)} %pos_ref.1) | copy-start | bytes 73732
  41.7 29.8 %copy-start.1 = (f32[3,2048]{1,0:T(4,128)S(1)}, f32[3,2048]{1,0:T(4,128)}, u32[]{:S(2)}) copy-start(f32[3,2048]{1,0:T(4,128)} %vel_ref.1) | copy-start | bytes 73732
  41.7 29.8 %copy-start.2 = (f32[3,2048]{1,0:T(4,128)S(1)}, f32[3,2048]{1,0:T(4,128)}, u32[]{:S(2)}) copy-start(f32[3,2048]{1,0:T(4,128)} %acc_ref.1) | copy-start | bytes 73732
  41.7 29.8 %copy-start.3 = (f32[3,2048]{1,0:T(4,128)S(1)}, f32[3,2048]{1,0:T(4,128)}, u32[]{:S(2)}) copy-start(f32[3,2048]{1,0:T(4,128)} %jrk_ref.1) | copy-start | bytes 73732
  65.6 5.9 %collective-permute-start.1 = (f32[16,128]{1,0:T(8,128)S(1)}, f32[16,128]{1,0:T(8,128)S(1)}, u32[]{:S(2)}, u32[]{:S(2)}) collective-permute-start(f32[16,128]{1,0:T(8,128)S(1)} %get-tuple-element.39.mine_ref), channel_id=1, source_target_pairs={{0,1},{1,0},{2,3},{3,2},{4,5},{5,4},{6,7},{7,6},{8,9},{9,8},{10,11... | collective-permute-start | bytes 24584 | tf_op jit(solution)/shard_map/ppermute | solution.py:424

commit v6 on v5

--- a/solution.py
+++ b/solution.py
@@ -126,7 +126,8 @@
     return (owner * (rows * LANES) + iota((rows, LANES), 0) * LANES + iota((rows, LANES), 1)).astype(F32)
 
 
-def prepare_kernel(source_ref, active_ref, first_hbm, factor_ref, moment_ref, perm_ref, first_ref, sent):
+def prepare_kernel(me_ref, source_ref, active_ref, first_hbm, factor_ref, moment_ref, perm_ref, select_ref,
+                   first_ref, sent):
     count = source_ref.shape[1]
     rows = active_ref.shape[0]
     total = rows * LANES
@@ -144,6 +145,12 @@
     first_ref[...] = jnp.sum(first, axis=0, keepdims=True).astype(jnp.int32)
     copy = pltpu.make_async_copy(first_ref, first_hbm, sent)
     copy.start()
+    first = jnp.sum(first, axis=0, keepdims=True)
+    start = jnp.sum(jnp.where(iota((1, LANES), 1) == me_ref[0], first, 0.0), axis=1, keepdims=True).astype(jnp.int32)
+    row, lane = iota((total // 2, LANES), 0), iota((total // 2, LANES), 1)
+    row = row + jnp.where(lane < SLOTS, 0, total // 2)
+    select = row - lax.bitwise_and(lane, SLOTS - 1) == start
+    select_ref[...] = jnp.where(select, 1.0, 0.0).astype(BF16)
     spots = iota((total, LANES), 0)
     for to in range(rows):
         rank = jnp.sum(ranks[to], axis=0, keepdims=True).astype(jnp.int32)
@@ -167,7 +174,7 @@
     copy.wait()
 
 
-def prepare(source, active):
+def prepare(me, source, active):
     count = source.shape[1]
     total = active.shape[0] * LANES
     return pl.pallas_call(
@@ -177,14 +184,15 @@
             jax.ShapeDtypeStruct((count, LANES), BF16),
             jax.ShapeDtypeStruct((32, count), BF16),
             jax.ShapeDtypeStruct((total, total), BF16),
+            jax.ShapeDtypeStruct((total // 2, LANES), BF16),
         ),
-        in_specs=[vmem()] * 2,
-        out_specs=(hbm(),) + (vmem(),) * 3,
+        in_specs=[smem()] + [vmem()] * 2,
+        out_specs=(hbm(),) + (vmem(),) * 4,
         scratch_shapes=[pltpu.VMEM((1, LANES), jnp.int32), pltpu.SemaphoreType.DMA],
         compiler_params=params(12),
         cost_estimate=cost(5),
         name="prepare",
-    )(source, active)
+    )(me, source, active)
 
 
 def place(first_ref, states_ref, compact, half, owner):
@@ -220,14 +228,12 @@
         for d in range(3):
             spread_ref[d, here, :] = wide[:, d * LANES:(d + 1) * LANES]
 
-    size = count // 8
-    spread(0, 4 * size)
+    wide, deep = 2, min(1024, count)
+    spread(0, deep)
     copy.wait()
 
-    spread(4 * size, 4 * size)
     for owner in range(owners):
         place(first_ref, states_ref, compact, 0, owner)
-    wide, deep = 2, min(1024, count)
     width = wide * LANES
 
     def part(block):
@@ -245,6 +251,8 @@
         radial = jnp.zeros((32, width), F32)
         for low in range(0, count, deep):
             here = slice(low, low + deep)
+            if block == 0 and low > 0:
+                spread(low, deep)
             rel = [jnp.concatenate([spread_ref[d, here, :]] * wide, axis=1) - x[d:d + 1] for d in range(3)]
             dist = rel[0] * rel[0] + rel[1] * rel[1] + (rel[2] * rel[2] + softening)
             inv = lax.rsqrt(dist)
@@ -303,7 +311,10 @@
 
 
 def repeat_kernel(value_ref, send_ref):
-    send_ref[...] = jnp.broadcast_to(value_ref[...][None], send_ref.shape)
+    for low in range(0, value_ref.shape[0], 8):
+        value = value_ref[low:low + 8]
+        for peer in range(send_ref.shape[0]):
+            send_ref[peer, low:low + 8, :] = value
 
 
 def repeat(value, peers):
@@ -317,9 +328,19 @@
     )(value)
 
 
+def add_rows(parts_ref, rows):
+    parts = [parts_ref[part, rows, :] for part in range(parts_ref.shape[0])]
+    while len(parts) > 1:
+        parts = [one + two for one, two in zip(parts[0::2], parts[1::2])]
+    return parts[0]
+
+
 def add_kernel(parts_ref, send_ref):
-    total = jnp.sum(parts_ref[...], axis=0)
-    send_ref[...] = jnp.broadcast_to(total[None], send_ref.shape)
+    for low in range(0, parts_ref.shape[1], 8):
+        rows = slice(low, low + 8)
+        total = add_rows(parts_ref, rows)
+        for peer in range(send_ref.shape[0]):
+            send_ref[peer, rows, :] = total
 
 
 def add_parts(parts, peers):
@@ -333,55 +354,52 @@
     )(parts)
 
 
-def correct_kernel(me_ref, first_ref, parts_ref, state_ref, own_ref, wide_ref):
+def correct_kernel(parts_ref, state_ref, select_ref, own_ref, terms_ref, wide):
     blocks = state_ref.shape[1]
-    total = jnp.sum(parts_ref[...], axis=0)
     tau = state_ref[6]
     t2 = tau * tau
     for d in range(3):
-        acc = total[d * blocks:(d + 1) * blocks]
-        jrk = total[(3 + d) * blocks:(4 + d) * blocks]
-        wide_ref[d, 0:blocks] = state_ref[d] + t2 * (0.15 * acc - tau * (jrk / 30.0))
-        wide_ref[3 + d, 0:blocks] = state_ref[3 + d] + tau * (0.5 * acc - tau * (jrk / 12.0))
-        wide_ref[6 + d, 0:blocks] = acc
-        wide_ref[9 + d, 0:blocks] = jrk
+        acc = add_rows(parts_ref, slice(d * blocks, (d + 1) * blocks))
+        jrk = add_rows(parts_ref, slice((3 + d) * blocks, (4 + d) * blocks))
+        wide[d] = state_ref[d] + t2 * (0.15 * acc - tau * (jrk / 30.0))
+        wide[3 + d] = state_ref[3 + d] + tau * (0.5 * acc - tau * (jrk / 12.0))
+        wide[6 + d] = acc
+        wide[9 + d] = jrk
     for f in range(12, 16):
-        wide_ref[f, 0:blocks] = jnp.ones_like(tau)
-    wide_ref[:, blocks:] = jnp.zeros((16, wide_ref.shape[1] - blocks, LANES), F32)
-    start = first_ref[0, me_ref[0]]
-    block = lax.shift_right_logical(start, 7)
-    shift = lax.bitwise_and(start, LANES - 1)
-    back = lax.bitwise_and(LANES - shift, LANES - 1)
-    lane = iota((16, LANES), 1)
-    low = pltpu.roll(wide_ref[:, block, :], back, 1)
-    high = pltpu.roll(wide_ref[:, block + 1, :], back, 1)
-    own_ref[...] = jnp.where(lane < LANES - shift, low, high)
-
-
-def correct(me, first, parts, state):
+        wide[f] = jnp.ones_like(tau)
+    value = jnp.concatenate([wide[:, block, :] for block in range(blocks)], axis=1)
+    terms = jnp.concatenate(three_terms(value), axis=0)
+    terms_ref[...] = terms
+    half = select_ref.shape[0]
+    low = jnp.dot(terms[:, 0:half], select_ref[...], preferred_element_type=F32)
+    high = jnp.dot(terms[:, half:2 * half], select_ref[...], preferred_element_type=F32)
+    low = low[0:16] + low[16:32] + low[32:48]
+    high = high[0:16] + high[16:32] + high[32:48]
+    own_ref[...] = low + pltpu.roll(high, SLOTS, 1)
+
+
+def correct(parts, state, select):
     blocks = state.shape[1]
     return pl.pallas_call(
         correct_kernel,
         out_shape=(
             jax.ShapeDtypeStruct((16, LANES), F32),
-            jax.ShapeDtypeStruct((16, blocks + 2, LANES), F32),
+            jax.ShapeDtypeStruct((48, blocks * LANES), BF16),
         ),
-        in_specs=[smem(), smem(), vmem(), vmem()],
+        in_specs=[vmem()] * 3,
         out_specs=(vmem(), vmem()),
+        scratch_shapes=[pltpu.VMEM((16, blocks, LANES), F32)],
         compiler_params=params(4),
         name="correct",
-    )(me, first, parts, state)
-
-
-def permute_kernel(wide_ref, perm_ref, update_ref):
-    blocks = perm_ref.shape[0] // LANES
-    value = jnp.concatenate([wide_ref[:, block, :] for block in range(blocks)], axis=1)
-    terms = jnp.concatenate(three_terms(value), axis=0)
-    result = jnp.dot(terms, perm_ref[...], preferred_element_type=F32)
+    )(parts, state, select)
+
+
+def permute_kernel(terms_ref, perm_ref, update_ref):
+    result = jnp.dot(terms_ref[...], perm_ref[...], preferred_element_type=F32)
     update_ref[...] = (result[0:16] + result[16:32] + result[32:48])[0:12]
 
 
-def permute(wide, perm):
+def permute(terms, perm):
     return pl.pallas_call(
         permute_kernel,
         out_shape=jax.ShapeDtypeStruct((12, perm.shape[1]), F32),
@@ -390,7 +408,7 @@
         compiler_params=params(8),
         cost_estimate=cost(2),
         name="permute",
-    )(wide, perm)
+    )(terms, perm)
 
 
 def write_kernel(mine_ref, other_ref, here_ref, there_ref, pos_ref, vel_ref, acc_ref, jrk_ref,
@@ -440,12 +458,12 @@
     column, late, mine = lax.optimization_barrier((column, active, mine))
     states = exchange(repeat(column, plane), PLANE).reshape(owners * ROWS, LANES)
     other = swap(mine)
-    first, factor, moment, perm = prepare(source, late)
-    states, other, perm = lax.optimization_barrier((states, other, perm))
+    first, factor, moment, perm, select = prepare(me, source, late)
+    states, other, perm, select = lax.optimization_barrier((states, other, perm, select))
     send, state = forces(first, states, factor, moment, blocks, plane)
     parts = exchange(add_parts(exchange(send, PLANE), depth), "z")
-    own, wide = correct(me, first, parts, state)
-    update = permute(wide, perm)
+    own, terms = correct(parts, state, select)
+    update = permute(terms, perm)
     new = write(own, swap(own), mine, other, position, velocity, accel, jerk_old)
     return new + (update,)
 

time: 72.9 us -> 72.5 us (level)
  no operation moved by 1% of the time
where the time goes in v6:
time: 72.5 us; the launch traced here: 72.1 us
  blocking collectives  38.7 us (53%)
  starting transfers between devices  14.2 us (20%)
  Pallas kernels  14.1 us (19%)
  waiting for transfers between devices  3.12 us (4%)
  local copies, waits for them, and re-layouts  1.22 us (2%)
  between operations  0.74 us (1%)
    all_to_all x3, blocking collectives, exchange(): return lax.all_to_all(value, axes, 0, 0, tiled=True)  38.7 us
    pallas_call x1, Pallas kernels, forces(): pl.pallas_call(force_kernel, out_shape=(jax.ShapeDtypeStruct((peers, 6 *...  7.57 us
    ppermute x2, starting transfers between devices, swap(): return lax.ppermute(value, 'core', [(0, 1), (1, 0)])  7.45 us
    all_to_all x1, starting transfers between devices, exchange(): return lax.all_to_all(value, axes, 0, 0, tiled=True)  6.75 us
    all_to_all x1, waiting for transfers between devices, exchange(): return lax.all_to_all(value, axes, 0, 0, tiled=True)  3.11 us
    pallas_call x1, Pallas kernels, prepare(): pl.pallas_call(prepare_kernel, out_shape=(jax.ShapeDtypeStruct((1, LANES)...  1.99 us
  transfers between devices with their start and end apart: 3, of which 1 were waited for; matrix products, arithmetic and copies ran while one was open for 0% of the time, Pallas kernels for 4%

profile of v6, /device:TPU:1, one launch (start us, length us, event | category | flops | bytes accessed | tf_op | source)
XLA Modules:
  0.0 72.1 jit_solution(536187955806401203)
XLA Ops:
  0.6 1.4 %pick.1 = (f32[56,128]{1,0:T(8,128)S(1)}, f32[8,2048]{1,0:T(8,128)S(1)}, s32[64,128]{1,0:T(8,128)S(1)}) custom-call(s32[1]{0:T(128)} %bitcast.me_ref, s32[8,128]{1,0:T(8,128)} %active_ref, f32[3,2048]{1,0:T(4,128)} %pos_ref.1, f32[3,2048]{1,0:T(4,128)} %vel_ref.1, f32[3,2048]{1,0:T(4,128)} %acc_ref.1, f32[3,2048]{1,0:T(4,128)} %jrk_ref.1, ...), custom_call_target="tpu_custom_call" | custom-call | tf_op jit(solution)/shard_map/pick/pallas_call | solution.py:107
  2.1 15.6 %all_to_all.20 = f32[8,7,1,128]{3,2,1,0:T(1,128)S(1)} all-to-all(f32[8,7,1,128]{3,2,1,0:T(1,128)S(1)} %bitcast.9), channel_id=1, replica_groups=mesh['z'=8,'y'=4,'x'=4,'core'=2] {'z'}, dimensions={0} | all-to-all | bytes 57344 | tf_op jit(solution)/shard_map/all_to_all | solution.py:446
  17.7 0.8 %repeat.1 = f32[16,56,128]{2,1,0:T(8,128)} custom-call(f32[56,128]{1,0:T(8,128)S(1)} %bitcast.8), custom_call_target="tpu_custom_call" | custom-call | tf_op jit(solution)/shard_map/repeat/pallas_call | solution.py:321
  18.5 6.8 %all-to-all-start.1 = ((f32[16,56,128]{2,1,0:T(8,128)}), f32[16,56,128]{2,1,0:T(8,128)S(1)}, u32[]{:S(2)}, u32[]{:S(2)}) async-start(f32[16,56,128]{2,1,0:T(8,128)} %repeat.1), calls=%async_computation.1 | async-start | bytes 917504 | tf_op jit(solution)/shard_map/all_to_all | solution.py:446
  25.3 2.5 %collective-permute-start = (s32[64,128]{1,0:T(8,128)S(1)}, s32[64,128]{1,0:T(8,128)S(1)}, u32[]{:S(2)}, u32[]{:S(2)}) collective-permute-start(s32[64,128]{1,0:T(8,128)S(1)} %get-tuple-element.34.here_ref), channel_id=1, source_target_pairs={{0,1},{1,0},{2,3},{3,2},{4,5},{5,4},{6,7},{7,6},{8,9},{9,8},{10,11... | collective-permute-start | bytes 98312 | tf_op jit(solution)/shard_map/ppermute | solution.py:442
  27.8 0.0 copy-start.4
  27.8 0.7 copy-done.4
  28.4 2.0 %prepare.1 = (s32[1,128]{1,0:T(1,128)S(1)}, bf16[2048,128]{1,0:T(8,128)(2,1)S(1)}, bf16[32,2048]{1,0:T(8,128)(2,1)S(1)}, bf16[1024,1024]{1,0:T(8,128)(2,1)S(1)}, bf16[512,128]{1,0:T(8,128)(2,1)S(1)}) custom-call(s32[1]{0:T(128)} %bitcast.me_ref, f32[8,2048]{1,0:T(8,128)S(1)} %get-tuple-element.28.source_ref, s32[8,128]{1,0:T(8,128)S(1)} %copy-done.4), custom_call_target="tpu_custom_call" | custom-call | bytes 15000000 | tf_op jit(solution)/shard_map/prepare/pallas_call | solution.py:180
  30.4 0.0 copy-start.5
  30.4 0.5 copy-done.5
  30.9 0.0 collective-permute-done.there_ref
  31.0 3.1 %all-to-all-done.1 = f32[16,56,128]{2,1,0:T(8,128)S(1)} async-done(((f32[16,56,128]{2,1,0:T(8,128)}), f32[16,56,128]{2,1,0:T(8,128)S(1)}, u32[]{:S(2)}, u32[]{:S(2)}) %all-to-all-start.1) | async-done | bytes 458784 | tf_op jit(solution)/shard_map/all_to_all | solution.py:446
  34.1 7.6 %forces.1 = (f32[16,48,128]{2,1,0:T(8,128)S(1)}, f32[8,8,128]{2,1,0:T(8,128)S(1)}) custom-call(s32[1,128]{1,0:T(1,128)} %copy-done.5, f32[896,128]{1,0:T(8,128)S(1)} %bitcast.7, bf16[2048,128]{1,0:T(8,128)(2,1)S(1)} %get-tuple-element.38.factor_ref, bf16[32,2048]{1,0:T(8,128)(2,1)S(1)} %get-tuple-element.39.moment_ref), custom_call_target="tpu_custom_call" | custom-call | bytes 27000000 | tf_op jit(solution)/shard_map/forces/pallas_call | solution.py:292
  41.6 0.0 copy-start
  41.7 0.0 copy-start.1
  41.7 0.0 copy-start.2
  41.7 0.0 copy-start.3
  41.7 11.9 %all_to_all.21.parts_ref = f32[16,48,128]{2,1,0:T(8,128)S(1)} all-to-all(f32[16,48,128]{2,1,0:T(8,128)S(1)} %get-tuple-element.40), channel_id=1, replica_groups=mesh['z'=8,'y'=4,'x'=4,'core'=2] {'y','x'}, dimensions={0} | all-to-all | bytes 786432 | tf_op jit(solution)/shard_map/all_to_all | solution.py:446
  53.6 11.1 %all_to_all.22.parts_ref = f32[8,48,128]{2,1,0:T(8,128)S(1)} all-to-all(f32[8,48,128]{2,1,0:T(8,128)S(1)} %add_parts.1), channel_id=1, replica_groups=mesh['z'=8,'y'=4,'x'=4,'core'=2] {'z'}, dimensions={0} | all-to-all | bytes 393216 | tf_op jit(solution)/shard_map/all_to_all | solution.py:446
  64.8 0.3 correct.1
  65.0 5.0 %collective-permute-start.1 = (f32[16,128]{1,0:T(8,128)S(1)}, f32[16,128]{1,0:T(8,128)S(1)}, u32[]{:S(2)}, u32[]{:S(2)}) collective-permute-start(f32[16,128]{1,0:T(8,128)S(1)} %get-tuple-element.43.mine_ref), channel_id=1, source_target_pairs={{0,1},{1,0},{2,3},{3,2},{4,5},{5,4},{6,7},{7,6},{8,9},{9,8},{10,11... | collective-permute-start | bytes 24584 | tf_op jit(solution)/shard_map/ppermute | solution.py:442
  70.0 1.1 %permute.1 = f32[12,1024]{1,0:T(8,128)} custom-call(bf16[48,1024]{1,0:T(8,128)(2,1)S(1)} %get-tuple-element.49.terms_ref, bf16[1024,1024]{1,0:T(8,128)(2,1)S(1)} %get-tuple-element.50.perm_ref), custom_call_target="tpu_custom_call" | custom-call | bytes 6000000 | tf_op jit(solution)/shard_map/permute/pallas_call | solution.py:403
  71.1 0.0 collective-permute-done.1.other_ref
  71.1 0.0 copy-done
  71.1 0.0 copy-done.1
  71.1 0.0 copy-done.2
  71.1 0.0 copy-done.3
  71.1 0.9 %write.1 = (f32[3,2048]{1,0:T(4,128)}, f32[3,2048]{1,0:T(4,128)}, f32[3,2048]{1,0:T(4,128)}, f32[3,2048]{1,0:T(4,128)}) custom-call(f32[16,128]{1,0:T(8,128)S(1)} %get-tuple-element.43.mine_ref, f32[16,128]{1,0:T(8,128)S(1)} %collective-permute-done.1.other_ref, s32[64,128]{1,0:T(8,128)S(1)} %get-tuple-element.34.here_ref, ...), custom_call_target="tpu_custom_call" | custom-call | tf_op jit(solution)/shard_map/write/pallas_call | solution.py:431
  (1 shorter events, 0.0 us)
Async XLA Ops:
  18.5 15.5 %all-to-all-start.1 = ((f32[16,56,128]{2,1,0:T(8,128)}), f32[16,56,128]{2,1,0:T(8,128)S(1)}, u32[]{:S(2)}, u32[]{:S(2)}) async-start(f32[16,56,128]{2,1,0:T(8,128)} %repeat.1), calls=%async_computation.1 | async-start | bytes 917504 | tf_op jit(solution)/shard_map/all_to_all | solution.py:446
  25.3 5.7 %collective-permute-start = (s32[64,128]{1,0:T(8,128)S(1)}, s32[64,128]{1,0:T(8,128)S(1)}, u32[]{:S(2)}, u32[]{:S(2)}) collective-permute-start(s32[64,128]{1,0:T(8,128)S(1)} %get-tuple-element.34.here_ref), channel_id=1, source_target_pairs={{0,1},{1,0},{2,3},{3,2},{4,5},{5,4},{6,7},{7,6},{8,9},{9,8},{10,11... | collective-permute-start | bytes 98312 | tf_op jit(solution)/shard_map/ppermute | solution.py:442
  27.8 0.7 copy-start.4
  30.4 0.5 copy-start.5
  41.6 29.5 %copy-start = (f32[3,2048]{1,0:T(4,128)S(1)}, f32[3,2048]{1,0:T(4,128)}, u32[]{:S(2)}) copy-start(f32[3,2048]{1,0:T(4,128)} %pos_ref.1) | copy-start | bytes 73732
  41.7 29.4 %copy-start.1 = (f32[3,2048]{1,0:T(4,128)S(1)}, f32[3,2048]{1,0:T(4,128)}, u32[]{:S(2)}) copy-start(f32[3,2048]{1,0:T(4,128)} %vel_ref.1) | copy-start | bytes 73732
  41.7 29.4 %copy-start.2 = (f32[3,2048]{1,0:T(4,128)S(1)}, f32[3,2048]{1,0:T(4,128)}, u32[]{:S(2)}) copy-start(f32[3,2048]{1,0:T(4,128)} %acc_ref.1) | copy-start | bytes 73732
  41.7 29.4 %copy-start.3 = (f32[3,2048]{1,0:T(4,128)S(1)}, f32[3,2048]{1,0:T(4,128)}, u32[]{:S(2)}) copy-start(f32[3,2048]{1,0:T(4,128)} %jrk_ref.1) | copy-start | bytes 73732
  65.0 6.1 %collective-permute-start.1 = (f32[16,128]{1,0:T(8,128)S(1)}, f32[16,128]{1,0:T(8,128)S(1)}, u32[]{:S(2)}, u32[]{:S(2)}) collective-permute-start(f32[16,128]{1,0:T(8,128)S(1)} %get-tuple-element.43.mine_ref), channel_id=1, source_target_pairs={{0,1},{1,0},{2,3},{3,2},{4,5},{5,4},{6,7},{7,6},{8,9},{9,8},{10,11... | collective-permute-start | bytes 24584 | tf_op jit(solution)/shard_map/ppermute | solution.py:442

commit v7 on v6

--- a/solution.py
+++ b/solution.py
@@ -55,7 +55,7 @@
     return lax.broadcasted_iota(jnp.int32, shape, axis)
 
 
-def pick_kernel(me_ref, active_hbm, *refs):
+def pick_kernel(active_hbm, *refs):
     inputs, send_ref, source_ref, place_ref = refs[0:7], refs[7], refs[8], refs[9]
     active_ref, kept, arrived = refs[10], refs[11:18], refs[18]
     copies = [pltpu.make_async_copy(active_hbm, active_ref, arrived.at[7])]
@@ -65,7 +65,7 @@
     count = kept[0].shape[1]
     rows = active_ref.shape[0]
     copies[0].wait()
-    offset = active_ref[...] - me_ref[0] * count
+    offset = active_ref[...] - lax.axis_index(SRC) * count
     owned = (offset >= 0) & (offset < count)
     flag = jnp.where(owned, 1.0, 0.0)
     before = jnp.where(iota((LANES, LANES), 0) < iota((LANES, LANES), 1), 1.0, 0.0)
@@ -101,7 +101,7 @@
     send_ref[...] = blocks
 
 
-def pick(me, position, velocity, accel, jerk_old, masses, phase, levels, active, peers):
+def pick(position, velocity, accel, jerk_old, masses, phase, levels, active, peers):
     count = position.shape[1]
     inputs = (position, velocity, accel, jerk_old, masses, phase, levels)
     return pl.pallas_call(
@@ -111,13 +111,13 @@
             jax.ShapeDtypeStruct((8, count), F32),
             jax.ShapeDtypeStruct((SLOTS, LANES), jnp.int32),
         ),
-        in_specs=[smem()] + [hbm()] * 8,
+        in_specs=[hbm()] * 8,
         out_specs=(vmem(), vmem(), vmem()),
         scratch_shapes=[pltpu.VMEM(value.shape, value.dtype) for value in (active,) + inputs]
         + [pltpu.SemaphoreType.DMA((8,))],
         compiler_params=params(8),
         name="pick",
-    )(me, pinned(active), *[pinned(value) for value in inputs])
+    )(pinned(active), *[pinned(value) for value in inputs])
 
 
 def sort_keys(active, count):
@@ -310,11 +310,12 @@
     )(pinned(first), states, factor, moment)
 
 
-def repeat_kernel(value_ref, send_ref):
-    for low in range(0, value_ref.shape[0], 8):
-        value = value_ref[low:low + 8]
-        for peer in range(send_ref.shape[0]):
-            send_ref[peer, low:low + 8, :] = value
+def repeat_kernel(value_ref, send_hbm, sent):
+    copies = [pltpu.make_async_copy(value_ref, send_hbm.at[peer], sent.at[peer]) for peer in range(send_hbm.shape[0])]
+    for copy in copies:
+        copy.start()
+    for copy in copies:
+        copy.wait()
 
 
 def repeat(value, peers):
@@ -322,7 +323,8 @@
         repeat_kernel,
         out_shape=jax.ShapeDtypeStruct((peers,) + value.shape, F32),
         in_specs=[vmem()],
-        out_specs=vmem(),
+        out_specs=hbm(),
+        scratch_shapes=[pltpu.SemaphoreType.DMA((peers,))],
         compiler_params=params(4),
         name="repeat",
     )(value)
@@ -451,7 +453,7 @@
     blocks = active.shape[0]
     me = lax.axis_index(SRC).reshape(1).astype(jnp.int32)
     send, source, mine = pick(
-        me, position, velocity, accel, jerk_old, masses.reshape(1, count), phase.reshape(1, count),
+        position, velocity, accel, jerk_old, masses.reshape(1, count), phase.reshape(1, count),
         levels.reshape(1, count), active, depth,
     )
     column = exchange(send.reshape(depth, ROWS, 1, LANES), "z").reshape(send.shape)

time: 72.5 us -> 72.6 us (level)
  no operation moved by 1% of the time
where the time goes in v7:
time: 72.6 us; the launch traced here: 72.2 us
  blocking collectives  38.7 us (53%)
  Pallas kernels  14.2 us (20%)
  starting transfers between devices  14.2 us (20%)
  waiting for transfers between devices  3.12 us (4%)
  local copies, waits for them, and re-layouts  1.22 us (2%)
  between operations  0.74 us (1%)
    all_to_all x3, blocking collectives, exchange(): return lax.all_to_all(value, axes, 0, 0, tiled=True)  38.7 us
    pallas_call x1, Pallas kernels, forces(): pl.pallas_call(force_kernel, out_shape=(jax.ShapeDtypeStruct((peers, 6 *...  7.57 us
    ppermute x2, starting transfers between devices, swap(): return lax.ppermute(value, 'core', [(0, 1), (1, 0)])  7.45 us
    all_to_all x1, starting transfers between devices, exchange(): return lax.all_to_all(value, axes, 0, 0, tiled=True)  6.77 us
    all_to_all x1, waiting for transfers between devices, exchange(): return lax.all_to_all(value, axes, 0, 0, tiled=True)  3.11 us
    pallas_call x1, Pallas kernels, prepare(): pl.pallas_call(prepare_kernel, out_shape=(jax.ShapeDtypeStruct((1, LANES)...  1.99 us
  transfers between devices with their start and end apart: 3, of which 1 were waited for; matrix products, arithmetic and copies ran while one was open for 0% of the time, Pallas kernels for 4%

profile of v7, /device:TPU:1, one launch (start us, length us, event | category | flops | bytes accessed | tf_op | source)
XLA Modules:
  0.0 72.2 jit_solution(18300065864670493893)
XLA Ops:
  0.6 1.4 %pick.1 = (f32[56,128]{1,0:T(8,128)S(1)}, f32[8,2048]{1,0:T(8,128)S(1)}, s32[64,128]{1,0:T(8,128)S(1)}) custom-call(s32[8,128]{1,0:T(8,128)} %active_ref, f32[3,2048]{1,0:T(4,128)} %pos_ref.1, f32[3,2048]{1,0:T(4,128)} %vel_ref.1, f32[3,2048]{1,0:T(4,128)} %acc_ref.1, f32[3,2048]{1,0:T(4,128)} %jrk_ref.1, f32[1,2048]{1,0:T(1,128)} %bitcast.10, ...), custom_call_target="tpu_custom_call" | custom-call | tf_op jit(solution)/shard_map/pick/pallas_call | solution.py:107
  2.1 15.6 %all_to_all.20 = f32[8,7,1,128]{3,2,1,0:T(1,128)S(1)} all-to-all(f32[8,7,1,128]{3,2,1,0:T(1,128)S(1)} %bitcast.9), channel_id=1, replica_groups=mesh['z'=8,'y'=4,'x'=4,'core'=2] {'z'}, dimensions={0} | all-to-all | bytes 57344 | tf_op jit(solution)/shard_map/all_to_all | solution.py:448
  17.7 0.9 %repeat.1 = f32[16,56,128]{2,1,0:T(8,128)} custom-call(f32[56,128]{1,0:T(8,128)S(1)} %bitcast.8), custom_call_target="tpu_custom_call" | custom-call | tf_op jit(solution)/shard_map/repeat/pallas_call | solution.py:322
  18.6 6.8 %all-to-all-start.1 = ((f32[16,56,128]{2,1,0:T(8,128)}), f32[16,56,128]{2,1,0:T(8,128)S(1)}, u32[]{:S(2)}, u32[]{:S(2)}) async-start(f32[16,56,128]{2,1,0:T(8,128)} %repeat.1), calls=%async_computation.1 | async-start | bytes 917504 | tf_op jit(solution)/shard_map/all_to_all | solution.py:448
  25.4 2.5 %collective-permute-start = (s32[64,128]{1,0:T(8,128)S(1)}, s32[64,128]{1,0:T(8,128)S(1)}, u32[]{:S(2)}, u32[]{:S(2)}) collective-permute-start(s32[64,128]{1,0:T(8,128)S(1)} %get-tuple-element.34.here_ref), channel_id=1, source_target_pairs={{0,1},{1,0},{2,3},{3,2},{4,5},{5,4},{6,7},{7,6},{8,9},{9,8},{10,11... | collective-permute-start | bytes 98312 | tf_op jit(solution)/shard_map/ppermute | solution.py:444
  27.9 0.0 copy-start.4
  27.9 0.7 copy-done.4
  28.6 2.0 %prepare.1 = (s32[1,128]{1,0:T(1,128)S(1)}, bf16[2048,128]{1,0:T(8,128)(2,1)S(1)}, bf16[32,2048]{1,0:T(8,128)(2,1)S(1)}, bf16[1024,1024]{1,0:T(8,128)(2,1)S(1)}, bf16[512,128]{1,0:T(8,128)(2,1)S(1)}) custom-call(s32[1]{0:T(128)} %bitcast.me_ref, f32[8,2048]{1,0:T(8,128)S(1)} %get-tuple-element.28.source_ref, s32[8,128]{1,0:T(8,128)S(1)} %copy-done.4), custom_call_target="tpu_custom_call" | custom-call | bytes 15000000 | tf_op jit(solution)/shard_map/prepare/pallas_call | solution.py:180
  30.6 0.0 copy-start.5
  30.6 0.5 copy-done.5
  31.1 0.0 collective-permute-done.there_ref
  31.1 3.1 %all-to-all-done.1 = f32[16,56,128]{2,1,0:T(8,128)S(1)} async-done(((f32[16,56,128]{2,1,0:T(8,128)}), f32[16,56,128]{2,1,0:T(8,128)S(1)}, u32[]{:S(2)}, u32[]{:S(2)}) %all-to-all-start.1) | async-done | bytes 458784 | tf_op jit(solution)/shard_map/all_to_all | solution.py:448
  34.2 7.6 %forces.1 = (f32[16,48,128]{2,1,0:T(8,128)S(1)}, f32[8,8,128]{2,1,0:T(8,128)S(1)}) custom-call(s32[1,128]{1,0:T(1,128)} %copy-done.5, f32[896,128]{1,0:T(8,128)S(1)} %bitcast.7, bf16[2048,128]{1,0:T(8,128)(2,1)S(1)} %get-tuple-element.38.factor_ref, bf16[32,2048]{1,0:T(8,128)(2,1)S(1)} %get-tuple-element.39.moment_ref), custom_call_target="tpu_custom_call" | custom-call | bytes 27000000 | tf_op jit(solution)/shard_map/forces/pallas_call | solution.py:292
  41.8 0.0 copy-start
  41.8 0.0 copy-start.1
  41.8 0.0 copy-start.2
  41.8 0.0 copy-start.3
  41.8 11.9 %all_to_all.21.parts_ref = f32[16,48,128]{2,1,0:T(8,128)S(1)} all-to-all(f32[16,48,128]{2,1,0:T(8,128)S(1)} %get-tuple-element.40), channel_id=1, replica_groups=mesh['z'=8,'y'=4,'x'=4,'core'=2] {'y','x'}, dimensions={0} | all-to-all | bytes 786432 | tf_op jit(solution)/shard_map/all_to_all | solution.py:448
  53.8 11.1 %all_to_all.22.parts_ref = f32[8,48,128]{2,1,0:T(8,128)S(1)} all-to-all(f32[8,48,128]{2,1,0:T(8,128)S(1)} %add_parts.1), channel_id=1, replica_groups=mesh['z'=8,'y'=4,'x'=4,'core'=2] {'z'}, dimensions={0} | all-to-all | bytes 393216 | tf_op jit(solution)/shard_map/all_to_all | solution.py:448
  64.9 0.3 correct.1
  65.2 5.0 %collective-permute-start.1 = (f32[16,128]{1,0:T(8,128)S(1)}, f32[16,128]{1,0:T(8,128)S(1)}, u32[]{:S(2)}, u32[]{:S(2)}) collective-permute-start(f32[16,128]{1,0:T(8,128)S(1)} %get-tuple-element.43.mine_ref), channel_id=1, source_target_pairs={{0,1},{1,0},{2,3},{3,2},{4,5},{5,4},{6,7},{7,6},{8,9},{9,8},{10,11... | collective-permute-start | bytes 24584 | tf_op jit(solution)/shard_map/ppermute | solution.py:444
  70.1 1.1 %permute.1 = f32[12,1024]{1,0:T(8,128)} custom-call(bf16[48,1024]{1,0:T(8,128)(2,1)S(1)} %get-tuple-element.49.terms_ref, bf16[1024,1024]{1,0:T(8,128)(2,1)S(1)} %get-tuple-element.50.perm_ref), custom_call_target="tpu_custom_call" | custom-call | bytes 6000000 | tf_op jit(solution)/shard_map/permute/pallas_call | solution.py:405
  71.2 0.0 collective-permute-done.1.other_ref
  71.2 0.0 copy-done
  71.2 0.0 copy-done.1
  71.2 0.0 copy-done.2
  71.2 0.0 copy-done.3
  71.3 0.9 %write.1 = (f32[3,2048]{1,0:T(4,128)}, f32[3,2048]{1,0:T(4,128)}, f32[3,2048]{1,0:T(4,128)}, f32[3,2048]{1,0:T(4,128)}) custom-call(f32[16,128]{1,0:T(8,128)S(1)} %get-tuple-element.43.mine_ref, f32[16,128]{1,0:T(8,128)S(1)} %collective-permute-done.1.other_ref, s32[64,128]{1,0:T(8,128)S(1)} %get-tuple-element.34.here_ref, ...), custom_call_target="tpu_custom_call" | custom-call | tf_op jit(solution)/shard_map/write/pallas_call | solution.py:433
  (1 shorter events, 0.0 us)
Async XLA Ops:
  18.6 15.6 %all-to-all-start.1 = ((f32[16,56,128]{2,1,0:T(8,128)}), f32[16,56,128]{2,1,0:T(8,128)S(1)}, u32[]{:S(2)}, u32[]{:S(2)}) async-start(f32[16,56,128]{2,1,0:T(8,128)} %repeat.1), calls=%async_computation.1 | async-start | bytes 917504 | tf_op jit(solution)/shard_map/all_to_all | solution.py:448
  25.4 5.7 %collective-permute-start = (s32[64,128]{1,0:T(8,128)S(1)}, s32[64,128]{1,0:T(8,128)S(1)}, u32[]{:S(2)}, u32[]{:S(2)}) collective-permute-start(s32[64,128]{1,0:T(8,128)S(1)} %get-tuple-element.34.here_ref), channel_id=1, source_target_pairs={{0,1},{1,0},{2,3},{3,2},{4,5},{5,4},{6,7},{7,6},{8,9},{9,8},{10,11... | collective-permute-start | bytes 98312 | tf_op jit(solution)/shard_map/ppermute | solution.py:444
  27.9 0.7 copy-start.4
  30.6 0.5 copy-start.5
  41.8 29.5 %copy-start = (f32[3,2048]{1,0:T(4,128)S(1)}, f32[3,2048]{1,0:T(4,128)}, u32[]{:S(2)}) copy-start(f32[3,2048]{1,0:T(4,128)} %pos_ref.1) | copy-start | bytes 73732
  41.8 29.5 %copy-start.1 = (f32[3,2048]{1,0:T(4,128)S(1)}, f32[3,2048]{1,0:T(4,128)}, u32[]{:S(2)}) copy-start(f32[3,2048]{1,0:T(4,128)} %vel_ref.1) | copy-start | bytes 73732
  41.8 29.4 %copy-start.2 = (f32[3,2048]{1,0:T(4,128)S(1)}, f32[3,2048]{1,0:T(4,128)}, u32[]{:S(2)}) copy-start(f32[3,2048]{1,0:T(4,128)} %acc_ref.1) | copy-start | bytes 73732
  41.8 29.4 %copy-start.3 = (f32[3,2048]{1,0:T(4,128)S(1)}, f32[3,2048]{1,0:T(4,128)}, u32[]{:S(2)}) copy-start(f32[3,2048]{1,0:T(4,128)} %jrk_ref.1) | copy-start | bytes 73732
  65.2 6.1 %collective-permute-start.1 = (f32[16,128]{1,0:T(8,128)S(1)}, f32[16,128]{1,0:T(8,128)S(1)}, u32[]{:S(2)}, u32[]{:S(2)}) collective-permute-start(f32[16,128]{1,0:T(8,128)S(1)} %get-tuple-element.43.mine_ref), channel_id=1, source_target_pairs={{0,1},{1,0},{2,3},{3,2},{4,5},{5,4},{6,7},{7,6},{8,9},{9,8},{10,11... | collective-permute-start | bytes 24584 | tf_op jit(solution)/shard_map/ppermute | solution.py:444
